TPU v7x, 32 devices: a whole 2x2x4 slice. The times are simulated.
32 devices in a mesh: dp: 8 (over z, x), mp: 4 (over y, core).
Axes of the slice: x: 2, y: 2, z: 4, core: 2. Of those that a mesh axis runs over, the one named last changes fastest.
Arguments:
- tokens: bfloat16 [8192, 1024], P(('dp', 'mp')), may hold values from -6 to 6
- segment_ids: int32 [32, 256], P('dp'), may hold values from 0 to 7, as said below
- gsd_index: int32 [32, 256], P('dp'), may hold values from 0 to 7, as said below
- enc_qkv: bfloat16 [3, 1024, 1024], P(None, None, 'mp'), may hold values from -0.1875 to 0.1875
- enc_qv_bias: float32 [2, 1024], P(None, 'mp'), may hold values from -1.75 to 1.75
- enc_out_proj: bfloat16 [1024, 1024], P('mp'), may hold values from -0.5 to 0.5
- enc_up: bfloat16 [1024, 4096], P(None, 'mp'), may hold values from -0.1875 to 0.1875
- enc_up_bias: float32 [4096], P('mp'), may hold values from -1.75 to 1.75
- enc_down: bfloat16 [4096, 1024], P('mp'), may hold values from -0.125 to 0.125
- enc_out_bias: float32 [2, 1024], replicated, may hold values from -1.75 to 1.75
- enc_gain: float32 [2, 1024], replicated, may hold values from 0.5 to 1.5
- enc_norm_bias: float32 [2, 1024], replicated, may hold values from -1.75 to 1.75
- embed_weight: bfloat16 [1024, 512], P(None, 'mp'), may hold values from -0.1875 to 0.1875
- embed_bias: float32 [512], replicated, may hold values from -1.75 to 1.75
- dec_qkv: bfloat16 [3, 512, 512], P(None, None, 'mp'), may hold values from -0.25 to 0.25
- dec_qv_bias: float32 [2, 512], P(None, 'mp'), may hold values from -1.75 to 1.75
- dec_out_proj: bfloat16 [512, 512], P('mp'), may hold values from -0.75 to 0.75
- dec_up: bfloat16 [512, 2048], P(None, 'mp'), may hold values from -0.25 to 0.25
- dec_up_bias: float32 [2048], P('mp'), may hold values from -1.75 to 1.75
- dec_down: bfloat16 [2048, 512], P('mp'), may hold values from -0.1875 to 0.1875
- dec_out_bias: float32 [2, 512], replicated, may hold values from -1.75 to 1.75
- dec_gain: float32 [2, 512], replicated, may hold values from 0.5 to 1.5
- dec_norm_bias: float32 [2, 512], replicated, may hold values from -1.75 to 1.75
- cotangent: bfloat16 [8192, 512], P(('dp', 'mp')), may hold values from -6 to 6
Outputs:
- output: float32 [8192, 512], P(('dp', 'mp'))
- grad_tokens: float32 [8192, 1024], P(('dp', 'mp'))
- grad_enc_qkv: float32 [3, 1024, 1024], P(None, None, 'mp')
- grad_enc_qv_bias: float32 [2, 1024], P(None, 'mp')
- grad_enc_out_proj: float32 [1024, 1024], P('mp')
- grad_enc_up: float32 [1024, 4096], P(None, 'mp')
- grad_enc_up_bias: float32 [4096], P('mp')
- grad_enc_down: float32 [4096, 1024], P('mp')
- grad_enc_out_bias: float32 [2, 1024], replicated
- grad_enc_gain: float32 [2, 1024], replicated
- grad_enc_norm_bias: float32 [2, 1024], replicated
- grad_embed_weight: float32 [1024, 512], P(None, 'mp')
- grad_embed_bias: float32 [512], replicated
- grad_dec_qkv: float32 [3, 512, 512], P(None, None, 'mp')
- grad_dec_qv_bias: float32 [2, 512], P(None, 'mp')
- grad_dec_out_proj: float32 [512, 512], P('mp')
- grad_dec_up: float32 [512, 2048], P(None, 'mp')
- grad_dec_up_bias: float32 [2048], P('mp')
- grad_dec_down: float32 [2048, 512], P('mp')
- grad_dec_out_bias: float32 [2, 512], replicated
- grad_dec_gain: float32 [2, 512], replicated
- grad_dec_norm_bias: float32 [2, 512], replicated
Inputs may be any that keep to these rules, and one draw needn't show every extreme that they name: `segment_ids`: in each row, images take consecutive positions numbered 1, 2, ... in order, each of 33 to 64 patches; 0 marks the padding after the last image. Some row holds the most images that fit. `gsd_index`: constant over the patches of one image; 0 on padding.
All inputs are finite; a program needn't handle non-finite values.
Results may differ from a plain program's by a relative error of at most 0.019.
Values may be sent and summed in bfloat16 or wider, within the bound.
No kernel may reach another device: no remote copies, remote signals or barrier semaphores. Data moves between devices by JAX's collectives and lax.ppermute only.
A program may use at most 128 MiB of HBM per device.

v0:
```python
import functools
import math

import jax
import jax.numpy as jnp
from jax import lax
from jax.experimental import pallas as pl
from jax.experimental.pallas import tpu as pltpu
from jax.sharding import PartitionSpec as P

HEADS = 16
DHEADS = 16
norm_eps = 1e-06
f32 = jnp.float32
bf16 = jnp.bfloat16
MIB = 1 << 20
VMEM = pl.BlockSpec(memory_space=pltpu.VMEM)
SMEM = pl.BlockSpec(memory_space=pltpu.SMEM)
COST = pl.CostEstimate(flops=10**10, bytes_accessed=10**8, transcendentals=0)


def shaped(dims, kind):
    return jax.ShapeDtypeStruct(dims, kind)


def kept(shape):
    return pltpu.HBM(shape.shape, shape.dtype)


def in_hbm(value):
    return pltpu.with_memory_space_constraint(value, pltpu.HBM)


class Chain:
    token = jax.ShapeDtypeStruct((8, 128), jnp.float32)

    def __init__(self):
        self.last = None

    def __call__(self, body, outs, args, smem=0, scratch=(), limit=16, prefetch=None, grid=None, specs=None):
        args, outs = list(args), list(outs)
        extra = self.last is not None
        ins = len(args) + (prefetch is not None)
        many = len(outs)

        def inner(*refs):
            out_refs = refs[ins + extra :]
            out_refs[many][...] = jnp.zeros((8, 128), f32)
            return body(*refs[:ins], *out_refs[:many], *out_refs[many + 1 :])

        if extra:
            args.append(self.last)
        tail = [pl.BlockSpec(memory_space=pl.ANY)] * extra
        params = pltpu.CompilerParams(vmem_limit_bytes=limit * MIB)
        if prefetch is None:
            got = pl.pallas_call(
                inner,
                out_shape=outs + [self.token],
                in_specs=[SMEM] * smem + [VMEM] * (len(args) - smem - extra) + tail,
                out_specs=[VMEM] * (many + 1),
                scratch_shapes=scratch,
                compiler_params=params,
                cost_estimate=COST,
            )(*args)
        else:
            got = pl.pallas_call(
                inner,
                out_shape=outs + [self.token],
                grid_spec=pltpu.PrefetchScalarGridSpec(
                    num_scalar_prefetch=1,
                    grid=grid,
                    in_specs=specs[0] + tail,
                    out_specs=specs[1] + [pl.BlockSpec((8, 128), lambda i, p: (0, 0))],
                ),
                compiler_params=params,
                cost_estimate=COST,
            )(prefetch, *args)
        *got, self.last = got
        return got

    def pin(self, value):
        def body(value_ref, last_ref, out_ref, token_ref):
            token_ref[...] = jnp.zeros((8, 128), f32)

        any_space = pl.BlockSpec(memory_space=pl.ANY)
        got, self.last = pl.pallas_call(
            body,
            out_shape=[shaped(value.shape, value.dtype), self.token],
            in_specs=[any_space, any_space],
            out_specs=[any_space, VMEM],
            input_output_aliases={0: 0},
            compiler_params=pltpu.CompilerParams(vmem_limit_bytes=MIB),
            cost_estimate=COST,
        )(value, self.last)
        return got

    def gap(self):
        self(lambda: None, [], [], limit=1)


def nn(a, b):
    return lax.dot_general(a, b, (((1,), (0,)), ((), ())), preferred_element_type=f32)


def nt(a, b):
    return lax.dot_general(a, b, (((1,), (1,)), ((), ())), preferred_element_type=f32)


def tn(a, b):
    return lax.dot_general(a, b, (((0,), (0,)), ((), ())), preferred_element_type=f32)


def swap(value, axis, mask):
    size = lax.axis_size(axis)
    return lax.ppermute(value, axis, [(i, i ^ mask) for i in range(size)])


def norm_parts(values):
    average = jnp.mean(values, axis=-1, keepdims=True)
    centred = values - average
    variance = jnp.mean(centred * centred, axis=-1, keepdims=True)
    scale = lax.rsqrt(variance + norm_eps)
    return centred * scale, scale


def norm_back(normal, scale, gain, grad):
    wide = grad * gain
    one = jnp.mean(wide, axis=-1, keepdims=True)
    two = jnp.mean(wide * normal, axis=-1, keepdims=True)
    return scale * (wide - one - normal * two)


def gelu_both(v):
    slope = math.sqrt(2.0 / math.pi)
    square = v * v
    t = jnp.tanh(slope * v * (1.0 + 0.044715 * square))
    half = 0.5 * (1.0 + t)
    return v * half, half + 0.5 * slope * v * (1.0 - t * t) * (1.0 + 3.0 * 0.044715 * square)


def sin_cos(x):
    turn = jnp.floor(x * (2.0 / math.pi) + 0.5)
    r = ((x - turn * 1.5703125) - turn * 4.837512969970703125e-4) - turn * 7.54978995489188216e-8
    z = r * r
    s = r + r * z * (-1.6666654611e-1 + z * (8.3321608736e-3 + z * -1.9515295891e-4))
    c = 1.0 - 0.5 * z + z * z * (
        4.166664568298827e-2 + z * (-1.388731625493765e-3 + z * 2.443315711809948e-5)
    )
    quarter = turn.astype(jnp.int32)
    odd = (quarter & 1) != 0
    sine = jnp.where(odd, c, s)
    cosine = jnp.where(odd, s, c)
    sine = jnp.where((quarter & 2) != 0, -sine, sine)
    cosine = jnp.where(((quarter + 1) & 2) != 0, -cosine, cosine)
    return sine, cosine


def head_masks(heads):
    size = 256 // heads
    lane = lax.broadcasted_iota(jnp.int32, (1, 256), 1)
    return [
        jnp.where((lane >= h * size) & (lane < (h + 1) * size), 1.0, 0.0).astype(bf16)
        for h in range(heads)
    ]


def attend(q, k, v, bias, heads, scale, keep):
    size = 256 // heads
    vt = v.astype(f32).T.astype(bf16)
    mixes = []
    for h, mask in enumerate(head_masks(heads)):
        s = nt(k, q * mask) + bias
        top = jnp.max(s, axis=0, keepdims=True)
        p = jnp.exp2((s - top) * (scale * math.log2(math.e)))
        total = jnp.sum(p, axis=0, keepdims=True)
        p = (p * (1.0 / total)).astype(bf16)
        keep(h, p)
        mixes.append(nn(vt[h * size : (h + 1) * size], p))
    return jnp.concatenate(mixes, axis=0).T


def attend_back(q, k, v, gm, probs, heads, scale):
    size = 256 // heads
    kt = k.astype(f32).T.astype(bf16)
    gq, gk, gv = [], 0.0, 0.0
    for h, mask in enumerate(head_masks(heads)):
        gmh = gm * mask
        p = probs(h)
        wide = p.astype(f32)
        t = wide * nt(v, gmh)
        gs = (t - wide * jnp.sum(t, axis=0, keepdims=True)).astype(bf16)
        gk = gk + nn(gs, q * mask)
        gv = gv + nn(p, gmh)
        gq.append(nn(kt[h * size : (h + 1) * size], gs))
    return jnp.concatenate(gq, axis=0).T * scale, gk * scale, gv


def place_of(slot, seg_ref, gsd_ref):
    n = seg_ref.shape[1]
    across = jnp.broadcast_to(seg_ref[pl.ds(slot, 1), :].astype(f32), (n, n))
    earlier = lax.broadcasted_iota(jnp.int32, (n, n), 1) < lax.broadcasted_iota(jnp.int32, (n, n), 0)
    rank = jnp.sum(jnp.where((across == across.T) & earlier, 1.0, 0.0), axis=1, keepdims=True)
    index = jnp.broadcast_to(gsd_ref[pl.ds(slot, 1), :].astype(f32), (n, n)).T[:, :1]
    return rank * (0.5 + 0.25 * index)


def start_body(slot_ref, seg_ref, gsd_ref, tokens_ref, gain_ref, shift_ref, wf_ref, normed_ref, stream_ref):
    place = place_of(slot_ref[0], seg_ref, gsd_ref)
    half = wf_ref.shape[1]
    sine, cosine = sin_cos(place * wf_ref[...])
    stream_ref[:, :half] = tokens_ref[:, :half].astype(f32) + sine
    stream_ref[:, half:] = tokens_ref[:, half:].astype(f32) + cosine
    normal, _ = norm_parts(stream_ref[...])
    normed_ref[...] = (normal * gain_ref[0:1] + shift_ref[0:1]).astype(bf16)


def mask_body(slot_ref, seg_ref, bias_a_ref, bias_b_ref):
    slot = slot_ref[0]
    n = seg_ref.shape[1]
    for j in range(4):
        across = jnp.broadcast_to(seg_ref[pl.ds(slot ^ j, 1), :].astype(f32), (n, n))
        (bias_a_ref, bias_b_ref)[j // 2][j % 2] = jnp.where(across == across.T, 0.0, -1e30)


def stream_body(slot_ref, seg_ref, gsd_ref, tokens_ref, eb_ref, wf_ref, nf_ref, pos_ref, stream_ref):
    place = place_of(slot_ref[0], seg_ref, gsd_ref)
    half = wf_ref.shape[1]
    sine, cosine = sin_cos(place * wf_ref[...])
    stream_ref[:, :half] = tokens_ref[:, :half].astype(f32) + sine
    stream_ref[:, half:] = tokens_ref[:, half:].astype(f32) + cosine
    half = nf_ref.shape[1]
    sine, cosine = sin_cos(place * nf_ref[...])
    pos_ref[:, :half] = sine + eb_ref[:, :half]
    pos_ref[:, half:] = cosine + eb_ref[:, half:]


def attn_body(scale, heads, first, *refs):
    count = (len(refs) - 9) // 2
    xs, rest = refs[:count], refs[count:]
    bias_ref, w_ref, qvb_ref, o_ref, q_ref, k_ref, v_ref, p_ref, mix_ref = rest[:9]
    for r, (x_ref, part_ref) in enumerate(zip(xs, rest[9:])):
        x = x_ref[...]
        q = (nn(x, w_ref[0]) + qvb_ref[0:1]).astype(bf16)
        k = nn(x, w_ref[1]).astype(bf16)
        v = (nn(x, w_ref[2]) + qvb_ref[1:2]).astype(bf16)
        q_ref[r], k_ref[r], v_ref[r] = q, k, v

        def keep(h, p):
            p_ref[r, h] = p

        mix = attend(q, k, v, bias_ref[first + r], heads, scale, keep).astype(bf16)
        mix_ref[r] = mix
        part_ref[...] = nn(mix, o_ref[...]).astype(bf16)


def attn_back_body(scale, heads, *refs):
    count = (len(refs) - 8) // 2
    gs, rest = refs[:count], refs[count:]
    q_ref, k_ref, v_ref, p_ref, w_ref, o_ref, g3_ref, sums_ref = rest[:8]
    total_q, total_v = 0.0, 0.0
    for r, (g_ref, part_ref) in enumerate(zip(gs, rest[8:])):
        gm = nt(g_ref[...], o_ref[...]).astype(bf16)
        gq, gk, gv = attend_back(
            q_ref[r], k_ref[r], v_ref[r], gm, lambda h: p_ref[r, h], heads, scale
        )
        total_q = total_q + jnp.sum(gq, axis=0, keepdims=True)
        total_v = total_v + jnp.sum(gv, axis=0, keepdims=True)
        acc = 0.0
        for c, g in enumerate((gq, gk, gv)):
            low = g.astype(bf16)
            g3_ref[r, :, c * 256 : (c + 1) * 256] = low
            acc = acc + nt(low, w_ref[c])
        part_ref[...] = acc.astype(bf16)
    sums_ref[0:1] = total_q
    sums_ref[1:2] = total_v


def mid_body(stream_ref, p_ref, near_ref, far_ref, ob_ref, gain_ref, shift_ref, mid_ref, normed_ref):
    total = p_ref[...].astype(f32) + near_ref[...].astype(f32) + far_ref[...].astype(f32)
    middle = stream_ref[...] + total + ob_ref[0:1]
    mid_ref[...] = middle
    normal, _ = norm_parts(middle)
    normed_ref[...] = (normal * gain_ref[1:2] + shift_ref[1:2]).astype(bf16)


def mlp_body(*refs):
    count = (len(refs) - 5) // 2
    xs, rest = refs[:count], refs[count:]
    up_ref, ub_ref, down_ref, hid_ref, dg_ref = rest[:5]
    width = up_ref.shape[1]
    for r, (x_ref, part_ref) in enumerate(zip(xs, rest[5:])):
        x = x_ref[...]
        for c in range(0, width, 256):
            cut = slice(c, c + 256)
            hidden, slope = gelu_both(nn(x, up_ref[:, cut]) + ub_ref[:, cut])
            hid_ref[r, :, cut] = hidden.astype(bf16)
            dg_ref[r, :, cut] = slope.astype(bf16)
        hidden = hid_ref[r]
        for c in range(0, down_ref.shape[1], 512):
            cut = slice(c, c + 512)
            part_ref[:, cut] = nn(hidden, down_ref[:, cut]).astype(bf16)


def mlp_back_body(*refs):
    count = (len(refs) - 5) // 2
    gs, rest = refs[:count], refs[count:]
    dg_ref, up_ref, down_ref, gp_ref, sums_ref = rest[:5]
    width = up_ref.shape[1]
    for r, (g_ref, part_ref) in enumerate(zip(gs, rest[5:])):
        g = g_ref[...]
        for c in range(0, width, 256):
            cut = slice(c, c + 256)
            grad = nt(g, down_ref[cut]) * dg_ref[r, :, cut].astype(f32)
            gp_ref[r, :, cut] = grad.astype(bf16)
            total = jnp.sum(grad, axis=0, keepdims=True)
            sums_ref[:, cut] = total if r == 0 else sums_ref[:, cut] + total
        gp = gp_ref[r]
        for c in range(0, up_ref.shape[0], 512):
            cut = slice(c, c + 512)
            part_ref[:, cut] = nt(gp, up_ref[cut]).astype(bf16)


def mlp_end_body(slot_ref, ge_ref, p_ref, near_ref, far_ref, mid_ref, gain_ref, ua_ref, ub_ref, uc_ref, dec_ref,
                 gmid_ref, gm_ref, pack_ref):
    slot = slot_ref[0]
    grad = p_ref[...].astype(f32) + near_ref[...].astype(f32) + far_ref[...].astype(f32)
    normal, scale = norm_parts(mid_ref[...])
    gmid = ge_ref[...] + norm_back(normal, scale, gain_ref[1:2], grad)
    gmid_ref[...] = gmid
    gm_ref[...] = gmid.astype(bf16)
    pack_ref[...] = jnp.zeros(pack_ref.shape, f32)
    pack_ref[0:1] = jnp.sum(gmid, axis=0, keepdims=True)
    pack_ref[1:2] = jnp.sum(grad * normal, axis=0, keepdims=True)
    pack_ref[2:3] = jnp.sum(grad, axis=0, keepdims=True)
    pack_ref[pl.ds(4 + slot, 1), :] = ua_ref[...] + ub_ref[...] + uc_ref[...]
    pack_ref[8:16] = dec_ref[...]


def last_body(slot_ref, gmid_ref, p_ref, near_ref, far_ref, stream_ref, gain_ref, sa_ref, sb_ref, sc_ref, mid_ref,
              gtok_ref, pack_ref):
    slot = slot_ref[0]
    grad = p_ref[...].astype(f32) + near_ref[...].astype(f32) + far_ref[...].astype(f32)
    normal, scale = norm_parts(stream_ref[...])
    gtok_ref[...] = gmid_ref[...] + norm_back(normal, scale, gain_ref[0:1], grad)
    pack_ref[:16] = mid_ref[...]
    pack_ref[16:] = jnp.zeros((8, pack_ref.shape[1]), f32)
    pack_ref[16:17] = jnp.sum(grad * normal, axis=0, keepdims=True)
    pack_ref[17:18] = jnp.sum(grad, axis=0, keepdims=True)
    share = sa_ref.shape[1]
    place = pl.ds(pl.multiple_of(slot * share, share), share)
    pack_ref[18:20, place] = sa_ref[...] + sb_ref[...] + sc_ref[...]


def decoder_body(slot_ref, mid_ref, p_ref, near_ref, far_ref, eob_ref, own_ref, by_ref, fa_ref, fb_ref, na_ref, nb_ref,
                 b0_ref, b1_ref, b2_ref, b3_ref, pos_ref, bias_ref, dob_ref, dgain_ref, dnb_ref, cot_ref,
                 encl_ref, out_ref, x1_ref, x2_ref, hid_ref, mix_ref, gp_ref, gm_ref, g3_ref, gz_ref,
                 gel_ref, ge_ref, sums_ref,
                 wup, wdown, wqkv, wout, wemb, pt, dg, qkv, wide, qvb_ref, upb_ref):
    slot, home = slot_ref[0], slot_ref[1]
    width = cot_ref.shape[1]
    block = width // 4
    heads = DHEADS * 256 // width
    groups = width // 256
    scale = (width // DHEADS) ** -0.5

    def place(j, base=0):
        return pl.ds(pl.multiple_of(base + (slot ^ j) * block, block), block)

    for j, ref in enumerate((b0_ref, b1_ref, b2_ref, b3_ref)):
        for c in range(2):
            qvb_ref[c : c + 1, j * block : (j + 1) * block] = ref[:, c * block : (c + 1) * block]
        upb_ref[:, j * width : (j + 1) * width] = ref[:, 2 * block :]
    piece, thin, tall = width // 8, block // 8, 2 * width // 8
    top = 2 * piece + thin
    step = top + piece + thin
    for j, (low_ref, high_ref) in enumerate(
        ((own_ref, own_ref), (by_ref, by_ref), (fa_ref, fb_ref), (na_ref, nb_ref))
    ):
        cut = slice(j * block, (j + 1) * block)
        for i in range(8):
            ref = (low_ref, high_ref)[i // 4]
            base = (i if j < 2 else i % 4) * step
            chunk = i if j < 2 else home ^ i

            def rows(size):
                return pl.ds(pl.multiple_of(chunk * size, size), size)

            wup[j, rows(piece)] = ref[base : base + piece]
            wdown[j, rows(piece)] = ref[base + piece : base + 2 * piece]
            wout[pl.ds(pl.multiple_of(j * block + chunk * thin, thin), thin)] = (
                ref[base + 2 * piece : base + top]
            )
            for c in range(3):
                wqkv[c, rows(piece), cut] = ref[base + top : base + top + piece, c * block : (c + 1) * block]
            wemb[pl.ds(pl.multiple_of(chunk * tall, tall), piece), cut] = (
                ref[base + top : base + top + piece, 3 * block :]
            )
            for c in range(4):
                wemb[pl.ds(pl.multiple_of(chunk * tall + piece + c * thin, thin), thin), cut] = (
                    ref[base + top + piece : base + step, c * block : (c + 1) * block]
                )
    encoded = mid_ref[...] + eob_ref[1:2]
    encoded = encoded + p_ref[...].astype(f32) + near_ref[...].astype(f32) + far_ref[...].astype(f32)
    encl_ref[...] = encoded.astype(bf16)
    embedded = nn(encl_ref[...], wemb[...])
    for j in range(4):
        wide[:, place(j)] = embedded[:, j * block : (j + 1) * block]
    stream = wide[...] + pos_ref[...]
    normal1, scale1 = norm_parts(stream)
    x1_ref[...] = (normal1 * dgain_ref[0:1] + dnb_ref[0:1]).astype(bf16)
    x1 = x1_ref[...]
    qkv[0] = (nn(x1, wqkv[0]) + qvb_ref[0:1]).astype(bf16)
    qkv[1] = nn(x1, wqkv[1]).astype(bf16)
    qkv[2] = (nn(x1, wqkv[2]) + qvb_ref[1:2]).astype(bf16)
    bias = bias_ref[0]
    for g in range(groups):
        cut = slice(g * 256, (g + 1) * 256)

        def keep(h, p):
            pt[g * heads + h] = p

        mix_ref[:, cut] = attend(
            qkv[0, :, cut], qkv[1, :, cut], qkv[2, :, cut], bias, heads, scale, keep
        ).astype(bf16)
    middle = stream + nn(mix_ref[...], wout[...]) + dob_ref[0:1]
    normal2, scale2 = norm_parts(middle)
    x2_ref[...] = (normal2 * dgain_ref[1:2] + dnb_ref[1:2]).astype(bf16)
    x2 = x2_ref[...]
    result = middle + dob_ref[1:2]
    for j in range(4):
        cut = slice(j * width, (j + 1) * width)
        hidden, slope = gelu_both(nn(x2, wup[j]) + upb_ref[:, cut])
        hid_ref[:, cut] = hidden.astype(bf16)
        dg[:, cut] = slope.astype(bf16)
        result = result + nn(hid_ref[:, cut], wdown[j])
    out_ref[...] = result

    cot = cot_ref[...]
    grad = 0.0
    sums_ref[...] = jnp.zeros(sums_ref.shape, f32)
    for j in range(4):
        cut = slice(j * width, (j + 1) * width)
        pre = nt(cot, wdown[j]) * dg[:, cut].astype(f32)
        gp_ref[:, cut] = pre.astype(bf16)
        block_sum = jnp.sum(pre, axis=0, keepdims=True)
        at = slot ^ j
        sums_ref[pl.ds(6 + (at >> 1), 1), pl.ds(pl.multiple_of((at & 1) * width, width), width)] = (
            block_sum
        )
        grad = grad + nt(gp_ref[:, cut], wup[j])
    cotf = cot.astype(f32)
    gmid = cotf + norm_back(normal2, scale2, dgain_ref[1:2], grad)
    gm_ref[...] = gmid.astype(bf16)
    sums_ref[1:2, :width] = jnp.sum(gmid, axis=0, keepdims=True)
    sums_ref[2:3, :width] = jnp.sum(cotf, axis=0, keepdims=True)
    sums_ref[2:3, width:] = jnp.sum(grad * normal2, axis=0, keepdims=True)
    sums_ref[4:5, :width] = jnp.sum(grad, axis=0, keepdims=True)
    gmix = nt(gm_ref[...], wout[...]).astype(bf16)
    grad = 0.0
    for g in range(groups):
        cut = slice(g * 256, (g + 1) * 256)
        three = attend_back(
            qkv[0, :, cut], qkv[1, :, cut], qkv[2, :, cut], gmix[:, cut],
            lambda h: pt[g * heads + h], heads, scale,
        )
        for c, part in enumerate(three):
            begin = c * width + g * 256
            low = part.astype(bf16)
            g3_ref[:, begin : begin + 256] = low
            grad = grad + nt(low, wqkv[c, :, cut])
        for c, row, base in ((0, 4, width), (2, 5, width)):
            total = jnp.sum(three[c], axis=0, keepdims=True)
            for i in range(256 // block):
                sums_ref[row : row + 1, place(g * (256 // block) + i, base)] = (
                    total[:, i * block : (i + 1) * block]
                )
    gstream = gmid + norm_back(normal1, scale1, dgain_ref[0:1], grad)
    sums_ref[3:4, width:] = jnp.sum(gstream, axis=0, keepdims=True)
    sums_ref[1:2, width:] = jnp.sum(grad * normal1, axis=0, keepdims=True)
    sums_ref[3:4, :width] = jnp.sum(grad, axis=0, keepdims=True)
    wide[...] = gstream
    for j in range(4):
        gz_ref[:, j * block : (j + 1) * block] = wide[:, place(j)].astype(bf16)
    ge = nt(gz_ref[...], wemb[...])
    ge_ref[...] = ge
    gel_ref[...] = ge.astype(bf16)
    sums_ref[0:1] = jnp.sum(ge, axis=0, keepdims=True)


def decoder_weights_body(x1_ref, x2_ref, hid_ref, mix_ref, gp_ref, gm_ref, g3_ref, gz_ref, encl_ref, cot_ref,
                         sent_ref, kept_ref):
    width = cot_ref.shape[1]
    block = width // 4
    cot, gm, x2 = cot_ref[...], gm_ref[...], x2_ref[...]
    piece, thin = width // 8, block // 8
    tall = encl_ref.shape[1] // 8
    top = 2 * piece + thin
    step = top + piece + thin

    def to(j):
        return sent_ref if j % 2 else kept_ref

    for j in (1, 3, 0, 2):
        w = to(j)
        i = j // 2
        cut = slice(j * width, (j + 1) * width)
        up = tn(x2, gp_ref[:, cut]).astype(bf16)
        down = tn(hid_ref[:, cut], cot).astype(bf16)
        out = tn(mix_ref[:, j * block : (j + 1) * block], gm).astype(bf16)
        for c in range(8):
            w[i, c * step : c * step + piece] = up[c * piece : (c + 1) * piece]
            w[i, c * step + piece : c * step + 2 * piece] = down[c * piece : (c + 1) * piece]
            w[i, c * step + 2 * piece : c * step + top] = out[c * thin : (c + 1) * thin]
    x1 = x1_ref[...]
    for k in range(3):
        full = tn(x1, g3_ref[:, k * width : (k + 1) * width]).astype(bf16)
        for j in range(4):
            for c in range(8):
                to(j)[j // 2, c * step + top : c * step + top + piece, k * block : (k + 1) * block] = (
                    full[c * piece : (c + 1) * piece, j * block : (j + 1) * block]
                )
    full = tn(encl_ref[...], gz_ref[...]).astype(bf16)
    for j in range(4):
        cut = slice(j * block, (j + 1) * block)
        for c in range(8):
            base = c * tall
            to(j)[j // 2, c * step + top : c * step + top + piece, 3 * block :] = full[base : base + piece, cut]
            base = base + piece
            for k in range(4):
                to(j)[j // 2, c * step + top + piece : (c + 1) * step, k * block : (k + 1) * block] = (
                    full[base + k * thin : base + (k + 1) * thin, cut]
                )


def pack_body(pick_ref, up_ref, down_ref, out_ref, qkv_ref, emb_ref, chunk_ref):
    piece, thin, block = up_ref.shape[0], out_ref.shape[0], emb_ref.shape[1]
    chunk_ref[:piece] = up_ref[...]
    chunk_ref[piece : 2 * piece] = down_ref[...]
    top = 2 * piece + thin
    chunk_ref[2 * piece : top] = out_ref[...]
    for c in range(3):
        chunk_ref[top : top + piece, c * block : (c + 1) * block] = qkv_ref[c]
    chunk_ref[top : top + piece, 3 * block :] = emb_ref[:piece]
    for c in range(4):
        base = piece + c * thin
        chunk_ref[top + piece :, c * block : (c + 1) * block] = emb_ref[base : base + thin]


def join_body(a_ref, b_ref, out_ref):
    rows = a_ref.shape[0]
    out_ref[:rows] = a_ref[...]
    out_ref[rows:] = b_ref[...]


def add_body(a_ref, b_ref, out_ref):
    out_ref[...] = (a_ref[...].astype(f32) + b_ref[...].astype(f32)).astype(out_ref.dtype)


def add_all_body(*refs):
    total = refs[0][...]
    for ref in refs[1:-1]:
        total = total + ref[...]
    refs[-1][...] = total


def last_sums_body(slot_ref, *refs):
    terms, outs, total_ref = refs[:-12], refs[-12:-1], refs[-1]
    total = terms[0][...]
    for ref in terms[1:]:
        total = total + ref[...]
    total_ref[...] = total
    slot = slot_ref[0]
    e_qv, e_upb, e_ob, e_gain, e_nb, d_emb, d_qv, d_upb, d_ob, d_gain, d_nb = outs
    share, thin, width = e_qv.shape[1], d_qv.shape[1], d_emb.shape[1]
    e_qv[...] = total_ref[18:20, pl.ds(pl.multiple_of(slot * share, share), share)]
    e_upb[...] = total_ref[pl.ds(4 + slot, 1), :]
    e_ob[0:1] = total_ref[0:1]
    e_ob[1:2] = total_ref[8:9]
    e_gain[0:1] = total_ref[16:17]
    e_gain[1:2] = total_ref[1:2]
    e_nb[0:1] = total_ref[17:18]
    e_nb[1:2] = total_ref[2:3]
    d_ob[...] = total_ref[9:11, :width]
    d_gain[...] = total_ref[9:11, width:]
    d_nb[...] = total_ref[11:13, :width]
    d_emb[...] = total_ref[11:12, width:]
    d_qv[...] = total_ref[12:14, pl.ds(pl.multiple_of(width + slot * thin, thin), thin)]
    d_upb[...] = total_ref[pl.ds(14 + (slot >> 1), 1), pl.ds(pl.multiple_of((slot & 1) * width, width), width)]


def halve_body(bit_ref, *refs):
    ins, (send_ref, keep_ref) = refs[:-2], refs[-2:]
    half = send_ref.shape[0]
    bit = bit_ref[0]
    for ref, which in ((send_ref, 1 - bit), (keep_ref, bit)):
        rows = pl.ds(pl.multiple_of(which * half, half), half)
        total = ins[0][rows].astype(f32)
        for other in ins[1:]:
            total = total + other[rows].astype(f32)
        ref[...] = total.astype(bf16)


def far_body(bit_ref, kept_ref, near_ref, out_ref):
    half = out_ref.shape[0]
    rows = pl.ds(pl.multiple_of(bit_ref[0] * half, half), half)
    out_ref[...] = (kept_ref[1, rows].astype(f32) + near_ref[1, rows].astype(f32)).astype(bf16)


def there_body(bit_ref, kept_ref, near_ref, far_ref, send_ref):
    half = send_ref.shape[0]
    rows = pl.ds(pl.multiple_of((1 - bit_ref[0]) * half, half), half)
    total = kept_ref[0, rows].astype(f32) + near_ref[0, rows].astype(f32)
    send_ref[...] = (total + far_ref[...].astype(f32)).astype(bf16)


def mine_body(bit_ref, kept_ref, near_ref, far_ref, got_ref, send_ref, keep_ref):
    quarter = send_ref.shape[0]
    base = bit_ref[0] * 2 * quarter
    for ref, which in ((send_ref, 1 - bit_ref[1]), (keep_ref, bit_ref[1])):
        rows = pl.ds(pl.multiple_of(base + which * quarter, quarter), quarter)
        inner = pl.ds(pl.multiple_of(which * quarter, quarter), quarter)
        total = kept_ref[0, rows].astype(f32) + near_ref[0, rows].astype(f32)
        ref[...] = (total + far_ref[inner].astype(f32) + got_ref[inner].astype(f32)).astype(bf16)


def piece_of(refs, j):
    for ref in refs:
        if len(ref.shape) == 2:
            if j == 0:
                return ref[...]
            j -= 1
        elif j < ref.shape[0]:
            return ref[j]
        else:
            j -= ref.shape[0]


def tile_sum(xs, gs, more):
    acc = 0.0
    for j in range(4):
        acc = acc + tn(piece_of(xs, j), piece_of(gs, j))
    if not more:
        return [(slice(None), slice(None), acc)]
    rows, cols = acc.shape
    parts = [(slice(None), slice(0, cols), acc)]
    half, quarter = rows // 2, rows // 8
    wide = more[0].shape[1] // 4
    for c in range(2):
        for k in range(4):
            parts.append((
                slice(c * half + k * quarter, c * half + (k + 1) * quarter),
                slice(cols, cols + wide),
                more[0][c * quarter : (c + 1) * quarter, k * wide : (k + 1) * wide].astype(f32),
            ))
    return parts


def first_half_body(nx, ng, nm, pick_ref, *refs):
    xs, gs, more = refs[:nx], refs[nx : nx + ng], refs[nx + ng : nx + ng + nm]
    out_ref = refs[nx + ng + nm]
    for rows, cols, value in tile_sum(xs, gs, more):
        out_ref[rows, cols] = value.astype(bf16)


def other_half_body(nx, ng, nm, pick_ref, *refs):
    xs, gs, more = refs[:nx], refs[nx : nx + ng], refs[nx + ng : nx + ng + nm]
    add_ref, send_ref, keep_ref = refs[nx + ng + nm :]
    parts = [
        (rows, cols, (value + add_ref[rows, cols].astype(f32)).astype(bf16))
        for rows, cols, value in tile_sum(xs, gs, more)
    ]

    def put(ref):
        for rows, cols, value in parts:
            ref[rows, cols] = value

    @pl.when(pl.program_id(0) == 0)
    def _():
        put(send_ref)

    @pl.when(pl.program_id(0) == 1)
    def _():
        put(keep_ref)


def weight_half(chain, xs, gs, more, cut, pick, add=None):
    tile = xs[0].shape[-1] // 4
    begin, cols = cut
    out_cols = cols + sum(m.shape[1] // 4 for m in more)

    def column(shape):
        lead = shape[:-1]
        return pl.BlockSpec(lead + (tile,), lambda i, p: (0,) * len(lead) + (p[i],))

    def whole(shape):
        lead = shape[:-1]
        return pl.BlockSpec(lead + (cols,), lambda i, p: (0,) * len(lead) + (begin // cols,))

    in_specs = [column(x.shape) for x in xs] + [whole(g.shape) for g in gs]
    in_specs += [pl.BlockSpec((tile // 4, m.shape[1]), lambda i, p: (p[i], 0)) for m in more]
    args = list(xs) + list(gs) + list(more)
    counts = len(xs), len(gs), len(more)
    if add is None:
        body = functools.partial(first_half_body, *counts)
        outs = [shaped((2 * tile, out_cols), bf16)]
        out_specs = [pl.BlockSpec((tile, out_cols), lambda i, p: (i, 0))]
    else:
        body = functools.partial(other_half_body, *counts)
        in_specs.append(pl.BlockSpec((tile, out_cols), lambda i, p: (p[2 + i], 0)))
        args.append(add)
        outs = [shaped((tile, out_cols), bf16)] * 2
        out_specs = [pl.BlockSpec((tile, out_cols), lambda i, p: (0, 0))] * 2
    return chain(body, outs, args, prefetch=pick, grid=(2,), specs=(in_specs, out_specs), limit=20)


def spread_body(writes, place_ref, *refs):
    sums = max(write[0] for write in writes) + 1
    out_refs = refs[2 * sums :]
    for i in range(8):
        for source, which, lead, first, every, row, rows, col, cols, at_col in writes:
            ref = refs[2 * source + i // 4]
            base = i % 4 * (ref.shape[0] // 4)
            at = place_ref[source] ^ i
            value = ref[base + row : base + row + rows, col : col + cols].astype(f32)
            to = pl.ds(pl.multiple_of(at * every + first, rows), rows)
            if lead is None:
                out_refs[which][to, at_col : at_col + cols] = value
            else:
                out_refs[which][lead, to] = value


def out_weight_body(*refs):
    mixes, gs, out_ref = refs[:3], refs[3:7], refs[7]
    acc = 0.0
    for j in range(4):
        acc = acc + tn(piece_of(mixes, j), piece_of(gs, j))
    out_ref[...] = acc.astype(bf16)


class Sum:
    def __init__(self, chain, masks=(1, 2, 4)):
        self.chain, self.masks = chain, masks
        self.size = lax.axis_size("dp")
        me = lax.axis_index("dp").astype(jnp.int32)
        b1, b2, b3 = self.bits = [jnp.where((me & mask) != 0, 1, 0).astype(jnp.int32) for mask in masks]
        self.place = 4 * b1 + 2 * b2 + b3 if self.size == 8 else jnp.int32(0)
        self.there = jnp.stack([2 * (1 - b1), 2 * (1 - b1) + 1])
        self.mine = jnp.stack([2 * b1 + 1 - b2, 2 * b1 + b2, 1 - b2, b2])
        steps = [self.second, self.third, self.fourth, self.fifth, self.sixth]
        self.steps = iter(steps if self.size == 8 else [])

    def step(self):
        for todo in self.steps:
            todo()
            return

    def product(self, xs, gs, more=(), cut=None):
        self.terms = (xs, gs, more, cut or (0, gs[0].shape[-1]))
        if self.size != 8:
            first = weight_half(self.chain, *self.terms, jnp.array([0, 1], jnp.int32))[0]
            other = weight_half(self.chain, *self.terms, jnp.array([2, 3], jnp.int32))[0]
            return self.general(jnp.concatenate([first, other], axis=0))
        self.got = swap(weight_half(self.chain, *self.terms, self.there)[0], "dp", self.masks[0])

    def shares(self, kept, near, there):
        self.terms = None
        self.held = (kept, near, there)
        if self.size == 8:
            half = shaped(there.shape, bf16)
            send = self.chain(there_body, [half], (self.bits[0].reshape(1), kept, near, there), smem=1)[0]
            self.got = swap(send, "dp", self.masks[0])

    def other(self, mine):
        kept, near, there = self.held
        self.held = (kept, near, mine)
        if self.size != 8:
            total = kept[0].astype(f32) + near[0].astype(f32)
            total = total + jnp.concatenate([mine, there], axis=0).astype(f32)
            self.general(total.astype(bf16))

    def second(self):
        if self.terms is None:
            rows, cols = self.got.shape
            half = shaped((rows // 2, cols), bf16)
            send, self.keep = self.chain(
                mine_body, [half, half], (jnp.stack(self.bits[:2]), *self.held, self.got), smem=1
            )
        else:
            send, self.keep = weight_half(self.chain, *self.terms, self.mine, self.got)
        self.got = swap(send, "dp", self.masks[1])

    def third(self):
        rows, cols = self.keep.shape
        half = shaped((rows // 2, cols), bf16)
        send, self.keep = self.chain(
            halve_body, [half, half], (self.bits[2].reshape(1), self.keep, self.got), smem=1
        )
        self.got = swap(send, "dp", self.masks[2])

    def fourth(self):
        self.keep = self.chain(add_body, [shaped(self.keep.shape, bf16)], (self.keep, self.got))[0]
        self.got = swap(self.keep, "dp", self.masks[2])

    def join(self):
        rows, cols = self.keep.shape
        self.keep = self.chain(join_body, [shaped((2 * rows, cols), bf16)], (self.keep, self.got))[0]

    def fifth(self):
        self.join()
        self.got = swap(self.keep, "dp", self.masks[1])

    def sixth(self):
        self.join()
        self.got = swap(self.keep, "dp", self.masks[0])

    def general(self, held):
        me = lax.axis_index("dp")
        bits = [1 << i for i in range(self.size.bit_length() - 1)]
        for bit in bits:
            mine = (me & bit) != 0
            half = held.shape[0] // 2
            other = lax.dynamic_slice_in_dim(held, jnp.where(mine, 0, half), half, 0)
            own = lax.dynamic_slice_in_dim(held, jnp.where(mine, half, 0), half, 0)
            held = (own.astype(f32) + swap(other, "dp", bit).astype(f32)).astype(bf16)
        for bit in reversed(bits):
            mine = (me & bit) != 0
            other = swap(held, "dp", bit)
            held = jnp.where(
                mine,
                jnp.concatenate([other, held], axis=0),
                jnp.concatenate([held, other], axis=0),
            )
        half = held.shape[0] // 2
        self.keep, self.got = held[:half], held[half:]


def per_device(
    tokens, segment_ids, gsd_index, enc_qkv, enc_qv_bias, enc_out_proj, enc_up, enc_up_bias,
    enc_down, enc_out_bias, enc_gain, enc_norm_bias, embed_weight, embed_bias, dec_qkv,
    dec_qv_bias, dec_out_proj, dec_up, dec_up_bias, dec_down, dec_out_bias, dec_gain,
    dec_norm_bias, cotangent,
):
    n, width = tokens.shape
    rows, length = segment_ids.shape
    assert rows == 4 and n == length == 256 and lax.axis_size("mp") == 4
    share, ff = enc_qkv.shape[2], enc_up.shape[1]
    dwidth, dff = cotangent.shape[1], dec_up.shape[1] * 4
    dshare = dwidth // 4
    heads = share // (width // HEADS)
    scale = (width // HEADS) ** -0.5
    slot = lax.axis_index("mp").astype(jnp.int32)
    at = slot.reshape(1)
    chain = Chain()
    dec = Sum(chain)
    home = dec.place

    def low(*dims):
        return shaped(dims, bf16)

    def full(*dims):
        return shaped(dims, f32)

    def waves(size):
        half = size // 2
        return jnp.power(10000.0, -jnp.arange(half, dtype=f32) / half).reshape(1, half)

    def near(value):
        return swap(value, "mp", 1)

    def far(value):
        return swap(value, "mp", 2)

    pack_rows = 3 * dwidth + 2 * dshare
    decoder_weights = [in_hbm(w) for w in (dec_up, dec_down, dec_out_proj, dec_qkv, embed_weight)]

    def pack(pick, steps):
        def block(shape):
            if len(shape) == 3:
                return pl.BlockSpec((shape[0], shape[1] // 8, shape[2]), lambda i, p: (0, p[i], 0))
            return pl.BlockSpec((shape[0] // 8, shape[1]), lambda i, p: (p[i], 0))

        rows = pack_rows // 8
        return chain(
            pack_body,
            [low(steps * rows, dwidth)],
            decoder_weights,
            prefetch=pick,
            grid=(steps,),
            specs=([block(w.shape) for w in decoder_weights], [pl.BlockSpec((rows, dwidth), lambda i, p: (i, 0))]),
        )[0]

    split = dec.size == 8
    got = far(pack(home.reshape(1), 1)) if split else None
    normed = chain(
        start_body,
        [low(n, width)],
        (at, in_hbm(segment_ids), in_hbm(gsd_index), in_hbm(tokens), in_hbm(enc_gain), in_hbm(enc_norm_bias), waves(width)),
        smem=1,
        scratch=[pltpu.VMEM((n, width), f32)],
    )[0]
    x = [normed, near(normed), far(normed)]
    bias_a, bias_b = chain(mask_body, [kept(full(2, n, n)), kept(full(2, n, n))], (at, in_hbm(segment_ids)), smem=1)

    def attention(bias, first, *blocks):
        count = len(blocks)
        return chain(
            functools.partial(attn_body, scale, heads, first),
            [kept(low(count, n, share))] * 3
            + [kept(low(count, heads, n, n)), kept(low(count, n, share))]
            + [low(n, width)] * count,
            (*blocks, bias, enc_qkv, enc_qv_bias, enc_out_proj),
        )

    def add(a, b):
        return chain(add_body, [shaped(a.shape, a.dtype)], (a, b))[0]

    def join(a, b):
        return chain(join_body, [low(a.shape[0] + b.shape[0], a.shape[1])], (a, b))[0]

    def both(blocks):
        blocks[2] = chain.pin(blocks[2])
        blocks.append(near(blocks[2]))

    *saved_a, mixa, part0, part1 = attention(bias_a, 0, x[0], x[1])
    part1 = near(part1)
    vector = jnp.concatenate([dec_qv_bias.reshape(-1), dec_up_bias]).reshape(1, -1)
    vectors = [vector, chain.pin(near(vector)), far(vector)]
    both(vectors)
    part1 = chain.pin(part1)
    if split:
        got = chain.pin(got)
        more = swap(got, "dp", 4)
    both(x)
    vectors[3] = chain.pin(vectors[3])
    chain.gap()
    *saved_d, mixd, part3 = attention(bias_b, 1, x[3])
    part3 = near(part3)
    *saved_c, mixc, part2 = attention(bias_b, 0, x[2])
    part2 = far(add(part2, part3))
    packed = pack(jnp.arange(8, dtype=jnp.int32), 8)
    packed_near = near(packed)
    pos, stream = chain(
        stream_body,
        [kept(full(n, dwidth)), full(n, width)],
        (at, in_hbm(segment_ids), in_hbm(gsd_index), in_hbm(tokens), in_hbm(embed_bias.reshape(1, -1)), waves(width), waves(dwidth)),
        smem=1,
    )
    if split:
        got = join(got, more)
        more = swap(got, "dp", 2)
    else:
        got = far(packed)
    middle, normed2 = chain(
        mid_body,
        [kept(full(n, width)), low(n, width)],
        (stream, part0, part1, part2, enc_out_bias, enc_gain, enc_norm_bias),
    )
    y = [normed2, near(normed2), far(normed2)]
    packed_near = chain.pin(packed_near)
    if split:
        got = join(got, more)
        more = swap(got, "dp", 1)
    else:
        more = got[pack_rows // 2 :]
        got = got[: pack_rows // 2]

    def feed(*blocks):
        count = len(blocks)
        return chain(
            mlp_body,
            [kept(low(count, n, ff))] * 2 + [low(n, width)] * count,
            (*blocks, enc_up, enc_up_bias.reshape(1, -1), enc_down),
        )

    hida, dga, part0, part1 = feed(y[0], y[1])
    part1 = near(part1)
    far_weights = [got, more]
    near_weights = [near(got)]
    both(y)
    part1 = chain.pin(part1)
    near_weights[0] = chain.pin(near_weights[0])
    hidd, dgd, part3 = feed(y[3])
    part3 = near(part3)
    hidc, dgc, part2 = feed(y[2])
    part2 = far(add(part2, part3))
    far_weights[1] = chain.pin(more)
    near_weights.append(near(far_weights[1]))
    part2 = chain.pin(part2)

    (enc_low, output, x1, x2, hid, mix, gp, gm, g3, gz, ge_low, ge, dec_sums) = chain(
        decoder_body,
        [kept(o) for o in (low(n, width), full(n, dwidth), low(n, dwidth), low(n, dwidth), low(n, dff),
                           low(n, dwidth), low(n, dff), low(n, dwidth), low(n, 3 * dwidth), low(n, dwidth))]
        + [low(n, width), kept(full(n, width)), kept(full(8, width))],
        (jnp.stack([slot, home]), middle, part0, part1, part2, enc_out_bias, packed, packed_near,
         *far_weights, *near_weights, *vectors, pos, bias_a, dec_out_bias, dec_gain,
         dec_norm_bias, cotangent),
        smem=1,
        scratch=[
            pltpu.VMEM((4, dwidth, dwidth), bf16), pltpu.VMEM((4, dwidth, dwidth), bf16),
            pltpu.VMEM((3, dwidth, dwidth), bf16), pltpu.VMEM((dwidth, dwidth), bf16),
            pltpu.VMEM((width, dwidth), bf16), pltpu.VMEM((DHEADS, n, n), bf16),
            pltpu.VMEM((n, dff), bf16), pltpu.VMEM((3, n, dwidth), bf16), pltpu.VMEM((n, dwidth), f32),
            pltpu.VMEM((2, dwidth), f32), pltpu.VMEM((1, dff), f32),
        ],
        limit=40,
    )
    g = [ge_low, near(ge_low), far(ge_low)]

    def feed_back(slope, *blocks):
        count = len(blocks)
        return chain(
            mlp_back_body,
            [kept(low(count, n, ff)), kept(full(1, ff))] + [low(n, width)] * count,
            (*blocks, slope, enc_up, enc_down),
        )

    def attention_back(saved, *blocks):
        count = len(blocks)
        return chain(
            functools.partial(attn_back_body, scale, heads),
            [kept(low(count, n, 3 * share)), kept(full(2, share))] + [low(n, width)] * count,
            (*blocks, *saved, enc_qkv, enc_out_proj),
        )

    def far_share(bit):
        return far(chain(far_body, [low(pack_rows // 2, dwidth)], (bit.reshape(1), kept_share, sent), smem=1)[0])

    def hbm(*values):
        return [in_hbm(v) for v in values]

    down, up, attn = Sum(chain), Sum(chain), Sum(chain)

    def finish(sums, outs, writes):
        return chain(
            functools.partial(spread_body, writes),
            [kept(full(*dims)) for dims in outs],
            (jnp.stack([f.place for f in sums]), *[v for f in sums for v in (f.keep, f.got)]),
            smem=1,
            limit=24,
        )

    chain.gap()
    gpa, upa, part0, part1 = feed_back(dga, g[0], g[1])
    part1 = near(part1)
    sent, kept_share = chain(
        decoder_weights_body,
        [low(2, pack_rows, dwidth), kept(low(2, pack_rows, dwidth))],
        (x1, x2, hid, mix, gp, gm, g3, gz, enc_low, cotangent),
        limit=24,
    )
    sent = near(sent)
    part1 = chain.pin(part1)
    both(g)
    gpc, upc, part2 = feed_back(dgc, g[2])
    gpd, upd, part3 = feed_back(dgd, g[3])
    part3 = near(part3)
    down.product(hbm(hida, hidc, hidd), g)
    part2 = far(add(part2, part3))
    chain.gap()
    grad_middle, gm_low, sums_mid = chain(
        mlp_end_body,
        [kept(full(n, width)), low(n, width), kept(full(16, width))],
        (at, ge, part0, part1, part2, middle, enc_gain, upa, upc, upd, dec_sums),
        smem=1,
    )
    m = [gm_low, near(gm_low), far(gm_low)]
    up.product(hbm(*y), hbm(gpa, gpc, gpd))
    g3a, sa, part0, part1 = attention_back(saved_a, m[0], m[1])
    part1 = near(part1)
    down.step()
    part1 = chain.pin(part1)
    there = far_share(1 - dec.bits[0])
    both(m)
    g3c, sc, part2 = attention_back(saved_c, m[2])
    out_full = chain(out_weight_body, [low(share, width)], (mixa, mixc, mixd, *m))[0]
    g3d, sd, part3 = attention_back(saved_d, m[3])
    part3 = near(part3)
    attn.product(hbm(*x), hbm(g3a, g3c, g3d), [out_full])
    part2 = far(add(part2, part3))
    down.step()
    up.step()
    dec.shares(kept_share, sent, there)
    down.step()
    grad_tokens, sums = chain(
        last_body,
        [kept(full(n, width)), full(24, width)],
        (at, grad_middle, part0, part1, part2, stream, enc_gain, sa, sc, sd, sums_mid),
        smem=1,
    )
    dec.other(far_share(dec.bits[0]))
    up.step()
    attn.step()
    down.step()
    up.step()
    attn.step()
    dec.step()
    hops = [("mp", 1), ("mp", 2)] + [("dp", 1 << i) for i in range(dec.size.bit_length() - 1)]
    hops = iter(hops)

    def hop(total, got=None):
        if got is not None:
            total = add(total, got)
        for axis, mask in hops:
            return total, swap(total, axis, mask)
        return total, None

    small = hop(sums)
    down.step()
    up.step()
    small = hop(*small)
    attn.step()
    dec.step()
    small = hop(*small)
    up.step()
    attn.step()
    dec.step()
    small = hop(*small)
    e_down = finish((down,), [(ff, width)], [(0, 0, None, 0, ff // 8, 0, ff // 8, 0, width, 0)])[0]
    attn.step()
    dec.step()
    small = hop(*small)
    e_up = finish((up,), [(width, ff)], [(0, 0, None, 0, width // 8, 0, width // 8, 0, ff, 0)])[0]
    while small[1] is not None:
        sums = small
        small = hop(*small)
    vectors = chain(
        last_sums_body,
        [full(2, share), full(1, ff), full(2, width), full(2, width), full(2, width), full(1, dwidth),
         full(2, dshare), full(1, dff // 4), full(2, dwidth), full(2, dwidth), full(2, dwidth)],
        (at, *sums),
        smem=1,
        scratch=[pltpu.VMEM((24, width), f32)],
    )
    dec.step()
    rows, fold = width // 8, share // 8
    e_qkv, e_out = finish(
        (attn,),
        [(3, width, share), (share, width)],
        [(0, 0, c, 0, rows, 0, rows, c * share, share, 0) for c in range(3)]
        + [(0, 1, None, 0, fold, k * fold, fold, 3 * share, width // 4, k * (width // 4)) for k in range(4)],
    )
    part, thin, tall = dwidth // 8, dshare // 8, width // 8
    top = 2 * part + thin
    d_up, d_down, d_out, d_qkv, e_embed = finish(
        (dec,),
        [(dwidth, dwidth), (dwidth, dwidth), (dshare, dwidth), (3, dwidth, dshare), (width, dshare)],
        [
            (0, 0, None, 0, part, 0, part, 0, dwidth, 0),
            (0, 1, None, 0, part, part, part, 0, dwidth, 0),
            (0, 2, None, 0, thin, 2 * part, thin, 0, dwidth, 0),
        ]
        + [(0, 3, c, 0, part, top, part, c * dshare, dshare, 0) for c in range(3)]
        + [(0, 4, None, 0, tall, top, part, 3 * dshare, dshare, 0)]
        + [(0, 4, None, part + k * thin, tall, top + part, thin, k * dshare, dshare, 0) for k in range(4)],
    )
    e_qv, e_upb, e_ob, e_gain, e_nb, d_emb, d_qv, d_upb, d_ob, d_gain, d_nb = vectors

    return (
        output,
        grad_tokens,
        e_qkv,
        e_qv,
        e_out,
        e_up,
        e_upb.reshape(-1),
        e_down,
        e_ob,
        e_gain,
        e_nb,
        e_embed,
        d_emb.reshape(-1),
        d_qkv,
        d_qv,
        d_out,
        d_up,
        d_upb.reshape(-1),
        d_down,
        d_ob,
        d_gain,
        d_nb,
    )


def solution(mesh):
    return jax.shard_map(
        per_device,
        mesh=mesh,
        in_specs=(
            P(("dp", "mp"), None),
            P("dp", None),
            P("dp", None),
            P(None, None, "mp"),
            P(None, "mp"),
            P("mp", None),
            P(None, "mp"),
            P("mp"),
            P("mp", None),
            P(),
            P(),
            P(),
            P(None, "mp"),
            P(),
            P(None, None, "mp"),
            P(None, "mp"),
            P("mp", None),
            P(None, "mp"),
            P("mp"),
            P("mp", None),
            P(),
            P(),
            P(),
            P(("dp", "mp"), None),
        ),
        out_specs=(
            P(("dp", "mp"), None),
            P(("dp", "mp"), None),
            P(None, None, "mp"),
            P(None, "mp"),
            P("mp", None),
            P(None, "mp"),
            P("mp"),
            P("mp", None),
            P(),
            P(),
            P(),
            P(None, "mp"),
            P(),
            P(None, None, "mp"),
            P(None, "mp"),
            P("mp", None),
            P(None, "mp"),
            P("mp"),
            P("mp", None),
            P(),
            P(),
            P(),
        ),
        check_vma=False,
    )
```

profile of v0, /device:TPU:0, one launch (start us, length us, event | category | flops | bytes accessed | tf_op | source)
XLA Modules:
  0.0 352.0 jit_solution(7114439480604910176)
XLA Ops:
  1.9 2.6 collective-permute-start.4
  5.4 2.4 shard_map.400
  8.4 1.8 collective-permute-start.1
  10.2 1.9 shard_map.401
  13.7 4.4 %shard_map.402 = (bf16[2,256,256]{2,1,0:T(8,128)(2,1)}, bf16[2,256,256]{2,1,0:T(8,128)(2,1)}, bf16[2,256,256]{2,1,0:T(8,128)(2,1)}, bf16[2,4,256,256]{3,2,1,0:T(...) custom-call(bf16[256,1024]{1,0:T(8,128)(2,1)S(1)} %get-tuple-element, ...), custom_call_target="tpu_custom_call" | custom-call | flops 10000000000 | bytes 100000000 | tf_op jit(solution)/shard_map/pallas_call | solution.py:56
  20.0 7.3 %collective-permute-done.1.value_ref = bf16[224,512]{1,0:T(8,128)(2,1)} collective-permute-done((bf16[224,512]{1,0:T(8,128)(2,1)S(1)}, bf16[224,512]{1,0:T(8,128)(2,1)}, u32[]{:S(2)}, u32[]{:S(2)}) %collective-permute-start.1) | collective-permute-done | bytes 229408 | tf_op jit(solution)/shard_map/ppermute | solution.py:115
  27.4 2.7 collective-permute-start.10
  31.1 2.4 shard_map.410
  33.7 3.5 shard_map.411
  37.9 5.1 %shard_map.413 = (bf16[1792,512]{1,0:T(8,128)(2,1)S(1)}, f32[8,128]{1,0:T(8,128)S(1)}) custom-call(s32[8]{0:T(128)S(1)} %iota.16.refs_0_, bf16[512,512]{1,0:T(8,128)(2,1)} %refs_1_.10, bf16[512,512]{1,0:T(8,128)(2,1)} %refs_2_.13, bf16[128,512]{1,0:T(8,128)(2,1)} %refs_3_.17, bf16[3,512,128]{2,1,0:T(8,128)(2,1)} %refs_4_.14, bf16[1024,128]{1,0:T(8,128)(2,1)} %refs_5_.11, ...), custom_call_target="tpu_custom_call" | custom-call | flops 10000000000 | bytes 100000000 | tf_op jit(solution)/shard_map/pallas_call | solution.py:66
  43.1 3.3 shard_map.414
  49.1 2.5 collective-permute-done.9.refs_3_
  53.3 7.0 %collective-permute-done.12.refs_1_ = bf16[448,512]{1,0:T(8,128)(2,1)S(1)} collective-permute-done((bf16[448,512]{1,0:T(8,128)(2,1)S(1)}, bf16[448,512]{1,0:T(8,128)(2,1)S(1)}, u32[]{:S(2)}, u32[]{:S(2)}) %collective-permute-start.12) | collective-permute-done | bytes 458784 | tf_op jit(solution)/shard_map/ppermute | solution.py:115
  62.6 4.3 %shard_map.419 = (bf16[2,256,1024]{2,1,0:T(8,128)(2,1)}, bf16[2,256,1024]{2,1,0:T(8,128)(2,1)}, bf16[256,1024]{1,0:T(8,128)(2,1)S(1)}, bf16[256,1024]{1,0:T(8,128)(2,1)S(1)}, f32[8,128]{1,0:T(8,128)S(1)}) custom-call(bf16[256,1024]{1,0:T(8,128)(2,1)S(1)} %get-tuple-element.292.refs_0_.refs_1_, bf16[256,1024]{1,0:T(8,128)(2,1)S(1)} %collective-permute-done.11.refs_1_.refs_2_, ...), custom_call_target="tpu_custom_call" | custom-call | flops 10000000000 | bytes 100000000 | tf_op jit(solution)/shard_map/pallas_call | solution.py:56
  69.6 2.5 shard_map.423
  72.2 2.5 shard_map.424
  76.4 6.9 %collective-permute-done.20.value_ref = bf16[896,512]{1,0:T(8,128)(2,1)S(1)} collective-permute-done((bf16[896,512]{1,0:T(8,128)(2,1)S(1)}, bf16[896,512]{1,0:T(8,128)(2,1)S(1)}, u32[]{:S(2)}, u32[]{:S(2)}) %collective-permute-start.20) | collective-permute-done | bytes 917536 | tf_op jit(solution)/shard_map/ppermute | solution.py:115
  83.3 5.8 %collective-permute-done.19.value_ref = bf16[256,1024]{1,0:T(8,128)(2,1)S(1)} collective-permute-done((bf16[256,1024]{1,0:T(8,128)(2,1)S(1)}, bf16[256,1024]{1,0:T(8,128)(2,1)S(1)}, u32[]{:S(2)}, u32[]{:S(2)}) %collective-permute-start.19) | collective-permute-done | bytes 524320 | tf_op jit(solution)/shard_map/ppermute | solution.py:115
  90.7 17.5 %shard_map.428 = (bf16[256,1024]{1,0:T(8,128)(2,1)}, f32[256,512]{1,0:T(8,128)}, bf16[256,512]{1,0:T(8,128)(2,1)}, bf16[256,512]{1,0:T(8,128)(2,1)}, bf16[256,20...) custom-call(s32[2]{0:T(128)S(1)} %pad_add_fusion.refs_0_, ...), custom_call_target="tpu_custom_call" | custom-call | flops 10000000000 | bytes 100000000 | tf_op jit(solution)/shard_map/pallas_call | solution.py:56
  111.1 3.2 shard_map.430
  114.5 4.2 %shard_map.431 = (bf16[2,1792,512]{2,1,0:T(8,128)(2,1)S(1)}, bf16[2,1792,512]{2,1,0:T(8,128)(2,1)}, f32[8,128]{1,0:T(8,128)S(1)}) custom-call(bf16[256,512]{1,0:T(8,128)(2,1)S(1)} %copy-done.42, bf16[256,512]{1,0:T(8,128)(2,1)S(1)} %copy-done.43, bf16[256,2048]{1,0:T(8,128)(2,1)S(1)} %copy-done.27, bf16[256,512]{1,0:T(8,128)(2,1)S(1)} %copy-done.44, ...), custom_call_target="tpu_custom_call" | custom-call | flops 10000000000 | bytes 100000000 | tf_op jit(solution)/shard_map/pallas_call | solution.py:56
  119.1 3.5 collective-permute-done.24.value_ref
  123.6 1.9 shard_map.434
  125.9 1.9 shard_map.435
  128.1 3.2 shard_map.436
  134.0 12.9 %collective-permute-done.27.refs_4_ = bf16[256,1024]{1,0:T(8,128)(2,1)S(1)} collective-permute-done((bf16[256,1024]{1,0:T(8,128)(2,1)S(1)}, bf16[256,1024]{1,0:T(8,128)(2,1)S(1)}, u32[]{:S(2)}, u32[]{:S(2)}) %collective-permute-start.27) | collective-permute-done | bytes 524320 | tf_op jit(solution)/shard_map/ppermute | solution.py:115
  146.9 2.0 shard_map.439
  150.1 3.9 %shard_map.440 = (bf16[512,1024]{1,0:T(8,128)(2,1)S(1)}, f32[8,128]{1,0:T(8,128)S(1)}) custom-call(s32[2]{0:T(128)S(1)} %pad_add_fusion.1.refs_0_, bf16[256,1024]{1,0:T(8,128)(2,1)} %copy-done.7, bf16[256,1024]{1,0:T(8,128)(2,1)} %copy-done.8, bf16[256,1024]{1,0:T(8,128)(2,1)} %copy-done.10, bf16[256,1024]{1,0:T(8,128)(2,1)} %copy-done.9, ...), custom_call_target="tpu_custom_call" | custom-call | flops 10000000000 | bytes 100000000 | tf_op jit(solution)/shard_map/pallas_call | solution.py:66
  154.5 4.7 %shard_map.441 = (bf16[2,256,768]{2,1,0:T(8,128)(2,1)}, f32[2,256]{1,0:T(2,128)}, bf16[256,1024]{1,0:T(8,128)(2,1)S(1)}, bf16[256,1024]{1,0:T(8,128)(2,1)S(1)}, f32[8,128]{1,0:T(8,128)S(1)}) custom-call(bf16[256,1024]{1,0:T(8,128)(2,1)S(1)} %get-tuple-element.361.refs_0_.refs_3_, bf16[256,1024]{1,0:T(8,128)(2,1)S(1)} %collective-permute-done.28.refs_1_.refs_4_, ...), custom_call_target="tpu_custom_call" | custom-call | flops 10000000000 | bytes 100000000 | tf_op jit(solution)/shard_map/pallas_call | solution.py:56
  159.2 3.5 shard_map.442
  164.4 2.0 copy-done.24
  167.9 2.5 shard_map.446
  171.6 2.6 shard_map.448
  174.3 3.5 %shard_map.449 = (bf16[512,1024]{1,0:T(8,128)(2,1)S(1)}, f32[8,128]{1,0:T(8,128)S(1)}) custom-call(s32[2]{0:T(128)S(1)} %pad_add_fusion.1.refs_0_, bf16[256,1024]{1,0:T(8,128)(2,1)} %copy-done.4, bf16[256,1024]{1,0:T(8,128)(2,1)} %copy-done.5, bf16[256,1024]{1,0:T(8,128)(2,1)} %get-tuple-element.273.refs_0_.refs_3_, bf16[256,1024]{1,0:T(8,128)(2,1)} %copy-done.6, ...), custom_call_target="tpu_custom_call" | custom-call | flops 10000000000 | bytes 100000000 | tf_op jit(solution)/shard_map/pallas_call | solution.py:66
  182.0 4.0 %shard_map.452 = (bf16[256,1024]{1,0:T(8,128)(2,1)S(1)}, bf16[256,1024]{1,0:T(8,128)(2,1)S(1)}, f32[8,128]{1,0:T(8,128)S(1)}) custom-call(s32[4]{0:T(128)S(1)} %pad_add_fusion.2.refs_0_, bf16[256,1024]{1,0:T(8,128)(2,1)} %copy-done.7, bf16[256,1024]{1,0:T(8,128)(2,1)} %copy-done.8, bf16[256,1024]{1,0:T(8,128)(2,1)} %copy-done.10, ...), custom_call_target="tpu_custom_call" | custom-call | flops 10000000000 | bytes 100000000 | tf_op jit(solution)/shard_map/pallas_call | solution.py:66
  186.5 3.6 %collective-permute-done.38.refs_3_ = bf16[896,512]{1,0:T(8,128)(2,1)S(1)} collective-permute-done((bf16[896,512]{1,0:T(8,128)(2,1)S(1)}, bf16[896,512]{1,0:T(8,128)(2,1)S(1)}, u32[]{:S(2)}, u32[]{:S(2)}) %collective-permute-start.38) | collective-permute-done | bytes 917536 | tf_op jit(solution)/shard_map/ppermute | solution.py:115
  190.5 1.7 collective-permute-start.50
  192.2 2.6 collective-permute-done.37.refs_1_
  195.0 5.8 %collective-permute-done.35.refs_4_ = bf16[256,1024]{1,0:T(8,128)(2,1)S(1)} collective-permute-done((bf16[256,1024]{1,0:T(8,128)(2,1)S(1)}, bf16[256,1024]{1,0:T(8,128)(2,1)S(1)}, u32[]{:S(2)}, u32[]{:S(2)}) %collective-permute-start.35) | collective-permute-done | bytes 524320 | tf_op jit(solution)/shard_map/ppermute | solution.py:115
  200.8 1.9 shard_map.455
  203.0 9.0 %collective-permute-done.41.refs_2_ = bf16[256,1024]{1,0:T(8,128)(2,1)S(1)} collective-permute-done((bf16[256,1024]{1,0:T(8,128)(2,1)S(1)}, bf16[256,1024]{1,0:T(8,128)(2,1)S(1)}, u32[]{:S(2)}, u32[]{:S(2)}) %collective-permute-start.41) | collective-permute-done | bytes 524320 | tf_op jit(solution)/shard_map/ppermute | solution.py:115
  212.2 4.0 %shard_map.458 = (bf16[256,1024]{1,0:T(8,128)(2,1)S(1)}, bf16[256,1024]{1,0:T(8,128)(2,1)S(1)}, f32[8,128]{1,0:T(8,128)S(1)}) custom-call(s32[4]{0:T(128)S(1)} %pad_add_fusion.2.refs_0_, bf16[256,1024]{1,0:T(8,128)(2,1)} %copy-done.4, bf16[256,1024]{1,0:T(8,128)(2,1)} %copy-done.5, bf16[256,1024]{1,0:T(8,128)(2,1)} %get-tuple-element.273.refs_0_.refs_3_, ...), custom_call_target="tpu_custom_call" | custom-call | flops 10000000000 | bytes 100000000 | tf_op jit(solution)/shard_map/pallas_call | solution.py:66
  217.7 2.0 collective-permute-start.48
  219.7 2.1 collective-permute-done.43.refs_1_
  221.9 11.2 %collective-permute-done.42.refs_2_ = bf16[256,1024]{1,0:T(8,128)(2,1)S(1)} collective-permute-done((bf16[256,1024]{1,0:T(8,128)(2,1)S(1)}, bf16[256,1024]{1,0:T(8,128)(2,1)S(1)}, u32[]{:S(2)}, u32[]{:S(2)}) %collective-permute-start.42) | collective-permute-done | bytes 524320 | tf_op jit(solution)/shard_map/ppermute | solution.py:115
  233.1 6.4 %collective-permute-start.47 = (bf16[128,1024]{1,0:T(8,128)(2,1)S(1)}, bf16[128,1024]{1,0:T(8,128)(2,1)S(1)}, u32[]{:S(2)}, u32[]{:S(2)}) collective-permute-start(bf16[128,1024]{1,0:T(8,128)(2,1)S(1)} %get-tuple-element.438.refs_0_), channel_id=1, source_target_pairs={{0,16},{4,20},{8,24},{12,28},{16,0},{20,4},{24,8},{28,12},{1,17},{... | collective-permute-start | bytes 786440 | tf_op jit(solution)/shard_map/ppermute | solution.py:115
  240.7 2.5 collective-permute-start.54
  243.3 11.8 %collective-permute-done.48.refs_1_ = bf16[256,1024]{1,0:T(8,128)(2,1)S(1)} collective-permute-done((bf16[256,1024]{1,0:T(8,128)(2,1)S(1)}, bf16[256,1024]{1,0:T(8,128)(2,1)S(1)}, u32[]{:S(2)}, u32[]{:S(2)}) %collective-permute-start.48) | collective-permute-done | bytes 524320 | tf_op jit(solution)/shard_map/ppermute | solution.py:115
  255.3 1.9 collective-permute-start.52
  257.9 2.9 collective-permute-start.51
  261.1 10.0 %collective-permute-done.54.refs_2_ = bf16[448,512]{1,0:T(8,128)(2,1)S(1)} collective-permute-done((bf16[448,512]{1,0:T(8,128)(2,1)S(1)}, bf16[448,512]{1,0:T(8,128)(2,1)S(1)}, u32[]{:S(2)}, u32[]{:S(2)}) %collective-permute-start.54) | collective-permute-done | bytes 458784 | tf_op jit(solution)/shard_map/ppermute | solution.py:115
  271.2 3.3 collective-permute-start.58
  274.9 13.7 %collective-permute-done.52.refs_1_ = bf16[256,1024]{1,0:T(8,128)(2,1)S(1)} collective-permute-done((bf16[256,1024]{1,0:T(8,128)(2,1)S(1)}, bf16[256,1024]{1,0:T(8,128)(2,1)S(1)}, u32[]{:S(2)}, u32[]{:S(2)}) %collective-permute-start.52) | collective-permute-done | bytes 524320 | tf_op jit(solution)/shard_map/ppermute | solution.py:115
  289.1 2.0 collective-permute-start.62
  291.1 2.3 shard_map.473
  293.3 9.5 %collective-permute-done.55.refs_1_ = bf16[256,1024]{1,0:T(8,128)(2,1)S(1)} collective-permute-done((bf16[256,1024]{1,0:T(8,128)(2,1)S(1)}, bf16[256,1024]{1,0:T(8,128)(2,1)S(1)}, u32[]{:S(2)}, u32[]{:S(2)}) %collective-permute-start.55) | collective-permute-done | bytes 524320 | tf_op jit(solution)/shard_map/ppermute | solution.py:115
  302.9 2.0 collective-permute-done.62.refs_1_
  306.2 2.0 collective-permute-done.64.refs_2_
  308.1 2.3 shard_map.477
  312.5 3.4 collective-permute-done.61.refs_1_
  317.4 14.5 %collective-permute-done.59.refs_2_ = bf16[512,1024]{1,0:T(8,128)(2,1)S(1)} collective-permute-done((bf16[512,1024]{1,0:T(8,128)(2,1)S(1)}, bf16[512,1024]{1,0:T(8,128)(2,1)S(1)}, u32[]{:S(2)}, u32[]{:S(2)}) %collective-permute-start.59) | collective-permute-done | bytes 1048608 | tf_op jit(solution)/shard_map/ppermute | solution.py:115
  331.9 2.3 shard_map.481
  334.2 15.3 %collective-permute-done.65.refs_2_ = bf16[896,512]{1,0:T(8,128)(2,1)S(1)} collective-permute-done((bf16[896,512]{1,0:T(8,128)(2,1)S(1)}, bf16[896,512]{1,0:T(8,128)(2,1)S(1)}, u32[]{:S(2)}, u32[]{:S(2)}) %collective-permute-start.65) | collective-permute-done | bytes 917536 | tf_op jit(solution)/shard_map/ppermute | solution.py:115
  349.5 2.1 shard_map.482
  (295 shorter events, 50.2 us)
Async XLA Ops:
  1.4 16.7 %collective-permute-start.5 = (f32[1,768]{1,0:T(1,128)S(1)}, f32[1,768]{1,0:T(1,128)S(1)}, u32[]{:S(2)}, u32[]{:S(2)}) collective-permute-start(f32[1,768]{1,0:T(1,128)S(1)} %reshape.113.refs_12_), channel_id=1, source_target_pairs={{0,1},{1,0},{2,3},{3,2},{4,5},{5,4},{6,7},{7,6},{8,9},{9,8},{10,11... | collective-permute-start | bytes 9224 | tf_op jit(solution)/shard_map/ppermute | solution.py:115
  1.9 16.2 %collective-permute-start.4 = (f32[1,768]{1,0:T(1,128)S(1)}, f32[1,768]{1,0:T(1,128)S(1)}, u32[]{:S(2)}, u32[]{:S(2)}) collective-permute-start(f32[1,768]{1,0:T(1,128)S(1)} %reshape.113.refs_12_), channel_id=1, source_target_pairs={{0,2},{1,3},{2,0},{3,1},{4,6},{5,7},{6,4},{7,5},{8,10},{9,11},{10,... | collective-permute-start | bytes 9224 | tf_op jit(solution)/shard_map/ppermute | solution.py:115
  7.9 4.5 %collective-permute-start.2 = (bf16[256,1024]{1,0:T(8,128)(2,1)S(1)}, bf16[256,1024]{1,0:T(8,128)(2,1)S(1)}, u32[]{:S(2)}, u32[]{:S(2)}) collective-permute-start(bf16[256,1024]{1,0:T(8,128)(2,1)S(1)} %get-tuple-element.262.refs_0_.refs_1_), channel_id=1, source_target_pairs={{0,1},{1,0},{2,3},{3,2},{4,5},{5,4},{6,7},{7,6},{8,9},{9,8},{10,11... | collective-permute-start | bytes 1572872 | tf_op jit(solution)/shard_map/ppermute | solution.py:115
  8.1 19.2 %collective-permute-start = (bf16[256,1024]{1,0:T(8,128)(2,1)S(1)}, bf16[256,1024]{1,0:T(8,128)(2,1)}, u32[]{:S(2)}, u32[]{:S(2)}) collective-permute-start(bf16[256,1024]{1,0:T(8,128)(2,1)S(1)} %get-tuple-element.262.refs_0_.refs_1_), channel_id=1, source_target_pairs={{0,2},{1,3},{2,0},{3,1},{4,6},{5,7},{6,4},{7,5},{8,10},{9,11},{10,... | collective-permute-start | bytes 1572872 | tf_op jit(solution)/shard_map/ppermute | solution.py:115
  8.4 18.9 %collective-permute-start.1 = (bf16[224,512]{1,0:T(8,128)(2,1)S(1)}, bf16[224,512]{1,0:T(8,128)(2,1)}, u32[]{:S(2)}, u32[]{:S(2)}) collective-permute-start(bf16[224,512]{1,0:T(8,128)(2,1)S(1)} %get-tuple-element.263), channel_id=1, source_target_pairs={{0,2},{1,3},{2,0},{3,1},{4,6},{5,7},{6,4},{7,5},{8,10},{9,11},{10,... | collective-permute-start | bytes 688136 | tf_op jit(solution)/shard_map/ppermute | solution.py:115
  18.1 11.9 %collective-permute-start.7 = (f32[1,768]{1,0:T(1,128)S(1)}, f32[1,768]{1,0:T(1,128)S(1)}, u32[]{:S(2)}, u32[]{:S(2)}) collective-permute-start(f32[1,768]{1,0:T(1,128)S(1)} %get-tuple-element.275.refs_14_), channel_id=1, source_target_pairs={{0,1},{1,0},{2,3},{3,2},{4,5},{5,4},{6,7},{7,6},{8,9},{9,8},{10,11... | collective-permute-start | bytes 9224 | tf_op jit(solution)/shard_map/ppermute | solution.py:115
  27.3 3.3 collective-permute-start.6
  27.4 19.0 %collective-permute-start.10 = (bf16[224,512]{1,0:T(8,128)(2,1)}, bf16[224,512]{1,0:T(8,128)(2,1)S(1)}, u32[]{:S(2)}, u32[]{:S(2)}) collective-permute-start(bf16[224,512]{1,0:T(8,128)(2,1)} %get-tuple-element.288.refs_0_), channel_id=1, source_target_pairs={{0,16},{4,20},{8,24},{12,28},{16,0},{20,4},{24,8},{28,12},{1,17},{... | collective-permute-start | bytes 688136 | tf_op jit(solution)/shard_map/ppermute | solution.py:115
  33.5 3.6 %collective-permute-start.8 = (bf16[256,1024]{1,0:T(8,128)(2,1)S(1)}, bf16[256,1024]{1,0:T(8,128)(2,1)S(1)}, u32[]{:S(2)}, u32[]{:S(2)}) collective-permute-start(bf16[256,1024]{1,0:T(8,128)(2,1)S(1)} %get-tuple-element.280), channel_id=1, source_target_pairs={{0,1},{1,0},{2,3},{3,2},{4,5},{5,4},{6,7},{7,6},{8,9},{9,8},{10,11... | collective-permute-start | bytes 1572872 | tf_op jit(solution)/shard_map/ppermute | solution.py:115
  37.3 14.2 %collective-permute-start.9 = (bf16[256,1024]{1,0:T(8,128)(2,1)S(1)}, bf16[256,1024]{1,0:T(8,128)(2,1)S(1)}, u32[]{:S(2)}, u32[]{:S(2)}) collective-permute-start(bf16[256,1024]{1,0:T(8,128)(2,1)S(1)} %get-tuple-element.287), channel_id=1, source_target_pairs={{0,2},{1,3},{2,0},{3,1},{4,6},{5,7},{6,4},{7,5},{8,10},{9,11},{10,... | collective-permute-start | bytes 1572872 | tf_op jit(solution)/shard_map/ppermute | solution.py:115
  43.0 10.4 %collective-permute-start.13 = (bf16[1792,512]{1,0:T(8,128)(2,1)S(1)}, bf16[1792,512]{1,0:T(8,128)(2,1)S(1)}, u32[]{:S(2)}, u32[]{:S(2)}) collective-permute-start(bf16[1792,512]{1,0:T(8,128)(2,1)S(1)} %get-tuple-element.294.refs_6_), channel_id=1, source_target_pairs={{0,1},{1,0},{2,3},{3,2},{4,5},{5,4},{6,7},{7,6},{8,9},{9,8},{10,11... | collective-permute-start | bytes 5505032 | tf_op jit(solution)/shard_map/ppermute | solution.py:115
  47.4 12.9 %collective-permute-start.12 = (bf16[448,512]{1,0:T(8,128)(2,1)S(1)}, bf16[448,512]{1,0:T(8,128)(2,1)S(1)}, u32[]{:S(2)}, u32[]{:S(2)}) collective-permute-start(bf16[448,512]{1,0:T(8,128)(2,1)S(1)} %get-tuple-element.293.refs_0_), channel_id=1, source_target_pairs={{0,8},{4,12},{8,0},{12,4},{16,24},{20,28},{24,16},{28,20},{1,9},{5... | collective-permute-start | bytes 1376264 | tf_op jit(solution)/shard_map/ppermute | solution.py:115
  52.8 9.2 %collective-permute-start.11 = (bf16[256,1024]{1,0:T(8,128)(2,1)S(1)}, bf16[256,1024]{1,0:T(8,128)(2,1)S(1)}, u32[]{:S(2)}, u32[]{:S(2)}) collective-permute-start(bf16[256,1024]{1,0:T(8,128)(2,1)S(1)} %get-tuple-element.292.refs_0_.refs_1_), channel_id=1, source_target_pairs={{0,1},{1,0},{2,3},{3,2},{4,5},{5,4},{6,7},{7,6},{8,9},{9,8},{10,11... | collective-permute-start | bytes 1572872 | tf_op jit(solution)/shard_map/ppermute | solution.py:115
  52.8 14.3 %collective-permute-start.15 = (bf16[256,1024]{1,0:T(8,128)(2,1)S(1)}, bf16[256,1024]{1,0:T(8,128)(2,1)S(1)}, u32[]{:S(2)}, u32[]{:S(2)}) collective-permute-start(bf16[256,1024]{1,0:T(8,128)(2,1)S(1)} %get-tuple-element.292.refs_0_.refs_1_), channel_id=1, source_target_pairs={{0,2},{1,3},{2,0},{3,1},{4,6},{5,7},{6,4},{7,5},{8,10},{9,11},{10,... | collective-permute-start | bytes 1572872 | tf_op jit(solution)/shard_map/ppermute | solution.py:115
  60.4 8.4 %collective-permute-start.17 = (bf16[896,512]{1,0:T(8,128)(2,1)S(1)}, bf16[896,512]{1,0:T(8,128)(2,1)S(1)}, u32[]{:S(2)}, u32[]{:S(2)}) collective-permute-start(bf16[896,512]{1,0:T(8,128)(2,1)S(1)} %get-tuple-element.304.refs_8_), channel_id=1, source_target_pairs={{0,1},{1,0},{2,3},{3,2},{4,5},{5,4},{6,7},{7,6},{8,9},{9,8},{10,11... | collective-permute-start | bytes 2752520 | tf_op jit(solution)/shard_map/ppermute | solution.py:115
  60.5 22.8 %collective-permute-start.20 = (bf16[896,512]{1,0:T(8,128)(2,1)S(1)}, bf16[896,512]{1,0:T(8,128)(2,1)S(1)}, u32[]{:S(2)}, u32[]{:S(2)}) collective-permute-start(bf16[896,512]{1,0:T(8,128)(2,1)S(1)} %get-tuple-element.304.refs_8_), channel_id=1, source_target_pairs={{0,4},{4,0},{8,12},{12,8},{16,20},{20,16},{24,28},{28,24},{1,5},{5... | collective-permute-start | bytes 2752520 | tf_op jit(solution)/shard_map/ppermute | solution.py:115
  66.9 1.9 collective-permute-start.14
  67.2 2.4 collective-permute-start.16
  72.0 2.6 collective-permute-start.18
  74.8 14.3 %collective-permute-start.19 = (bf16[256,1024]{1,0:T(8,128)(2,1)S(1)}, bf16[256,1024]{1,0:T(8,128)(2,1)S(1)}, u32[]{:S(2)}, u32[]{:S(2)}) collective-permute-start(bf16[256,1024]{1,0:T(8,128)(2,1)S(1)} %get-tuple-element.311), channel_id=1, source_target_pairs={{0,2},{1,3},{2,0},{3,1},{4,6},{5,7},{6,4},{7,5},{8,10},{9,11},{10,... | collective-permute-start | bytes 1572872 | tf_op jit(solution)/shard_map/ppermute | solution.py:115
  83.3 5.9 %collective-permute-start.21 = (bf16[896,512]{1,0:T(8,128)(2,1)S(1)}, bf16[896,512]{1,0:T(8,128)(2,1)S(1)}, u32[]{:S(2)}, u32[]{:S(2)}) collective-permute-start(bf16[896,512]{1,0:T(8,128)(2,1)S(1)} %get-tuple-element.316.refs_9_), channel_id=1, source_target_pairs={{0,1},{1,0},{2,3},{3,2},{4,5},{5,4},{6,7},{7,6},{8,9},{9,8},{10,11... | collective-permute-start | bytes 2752520 | tf_op jit(solution)/shard_map/ppermute | solution.py:115
  108.2 14.3 %collective-permute-start.24 = (bf16[256,1024]{1,0:T(8,128)(2,1)S(1)}, bf16[256,1024]{1,0:T(8,128)(2,1)S(1)}, u32[]{:S(2)}, u32[]{:S(2)}) collective-permute-start(bf16[256,1024]{1,0:T(8,128)(2,1)S(1)} %get-tuple-element.324.refs_0_.refs_4_), channel_id=1, source_target_pairs={{0,2},{1,3},{2,0},{3,1},{4,6},{5,7},{6,4},{7,5},{8,10},{9,11},{10,... | collective-permute-start | bytes 1572872 | tf_op jit(solution)/shard_map/ppermute | solution.py:115
  114.3 4.8 %collective-permute-start.23 = (bf16[256,1024]{1,0:T(8,128)(2,1)S(1)}, bf16[256,1024]{1,0:T(8,128)(2,1)S(1)}, u32[]{:S(2)}, u32[]{:S(2)}) collective-permute-start(bf16[256,1024]{1,0:T(8,128)(2,1)S(1)} %get-tuple-element.328), channel_id=1, source_target_pairs={{0,1},{1,0},{2,3},{3,2},{4,5},{5,4},{6,7},{7,6},{8,9},{9,8},{10,11... | collective-permute-start | bytes 1572872 | tf_op jit(solution)/shard_map/ppermute | solution.py:115
  118.7 45.6 %collective-permute-start.32 = (bf16[2,1792,512]{2,1,0:T(8,128)(2,1)S(1)}, bf16[2,1792,512]{2,1,0:T(8,128)(2,1)S(1)}, u32[]{:S(2)}, u32[]{:S(2)}) collective-permute-start(bf16[2,1792,512]{2,1,0:T(8,128)(2,1)S(1)} %get-tuple-element.378), channel_id=1, source_target_pairs={{0,1},{1,0},{2,3},{3,2},{4,5},{5,4},{6,7},{7,6},{8,9},{9,8},{10,11... | collective-permute-start | bytes 11010056 | tf_op jit(solution)/shard_map/ppermute | solution.py:115
  122.6 3.3 collective-permute-start.25
  127.8 5.2 %collective-permute-start.26 = (bf16[256,1024]{1,0:T(8,128)(2,1)S(1)}, bf16[256,1024]{1,0:T(8,128)(2,1)S(1)}, u32[]{:S(2)}, u32[]{:S(2)}) collective-permute-start(bf16[256,1024]{1,0:T(8,128)(2,1)S(1)} %get-tuple-element.348), channel_id=1, source_target_pairs={{0,1},{1,0},{2,3},{3,2},{4,5},{5,4},{6,7},{7,6},{8,9},{9,8},{10,11... | collective-permute-start | bytes 1572872 | tf_op jit(solution)/shard_map/ppermute | solution.py:115
  131.3 27.9 %collective-permute-start.30 = (bf16[512,1024]{1,0:T(8,128)(2,1)S(1)}, bf16[512,1024]{1,0:T(8,128)(2,1)S(1)}, u32[]{:S(2)}, u32[]{:S(2)}) collective-permute-start(bf16[512,1024]{1,0:T(8,128)(2,1)S(1)} %get-tuple-element.373), channel_id=1, source_target_pairs={{0,4},{4,0},{8,12},{12,8},{16,20},{20,16},{24,28},{28,24},{1,5},{5... | collective-permute-start | bytes 3145736 | tf_op jit(solution)/shard_map/ppermute | solution.py:115
  133.1 13.8 %collective-permute-start.27 = (bf16[256,1024]{1,0:T(8,128)(2,1)S(1)}, bf16[256,1024]{1,0:T(8,128)(2,1)S(1)}, u32[]{:S(2)}, u32[]{:S(2)}) collective-permute-start(bf16[256,1024]{1,0:T(8,128)(2,1)S(1)} %get-tuple-element.354), channel_id=1, source_target_pairs={{0,2},{1,3},{2,0},{3,1},{4,6},{5,7},{6,4},{7,5},{8,10},{9,11},{10,... | collective-permute-start | bytes 1572872 | tf_op jit(solution)/shard_map/ppermute | solution.py:115
  148.9 5.5 %collective-permute-start.28 = (bf16[256,1024]{1,0:T(8,128)(2,1)S(1)}, bf16[256,1024]{1,0:T(8,128)(2,1)S(1)}, u32[]{:S(2)}, u32[]{:S(2)}) collective-permute-start(bf16[256,1024]{1,0:T(8,128)(2,1)S(1)} %get-tuple-element.361.refs_0_.refs_3_), channel_id=1, source_target_pairs={{0,1},{1,0},{2,3},{3,2},{4,5},{5,4},{6,7},{7,6},{8,9},{9,8},{10,11... | collective-permute-start | bytes 1572872 | tf_op jit(solution)/shard_map/ppermute | solution.py:115
  148.9 17.7 %collective-permute-start.31 = (bf16[256,1024]{1,0:T(8,128)(2,1)S(1)}, bf16[256,1024]{1,0:T(8,128)(2,1)S(1)}, u32[]{:S(2)}, u32[]{:S(2)}) collective-permute-start(bf16[256,1024]{1,0:T(8,128)(2,1)S(1)} %get-tuple-element.361.refs_0_.refs_3_), channel_id=1, source_target_pairs={{0,2},{1,3},{2,0},{3,1},{4,6},{5,7},{6,4},{7,5},{8,10},{9,11},{10,... | collective-permute-start | bytes 1572872 | tf_op jit(solution)/shard_map/ppermute | solution.py:115
  154.0 28.0 %collective-permute-start.39 = (bf16[512,1024]{1,0:T(8,128)(2,1)S(1)}, bf16[512,1024]{1,0:T(8,128)(2,1)S(1)}, u32[]{:S(2)}, u32[]{:S(2)}) collective-permute-start(bf16[512,1024]{1,0:T(8,128)(2,1)S(1)} %get-tuple-element.415), channel_id=1, source_target_pairs={{0,4},{4,0},{8,12},{12,8},{16,20},{20,16},{24,28},{28,24},{1,5},{5... | collective-permute-start | bytes 3145736 | tf_op jit(solution)/shard_map/ppermute | solution.py:115
  159.2 5.2 %collective-permute-start.29 = (bf16[256,1024]{1,0:T(8,128)(2,1)S(1)}, bf16[256,1024]{1,0:T(8,128)(2,1)S(1)}, u32[]{:S(2)}, u32[]{:S(2)}) collective-permute-start(bf16[256,1024]{1,0:T(8,128)(2,1)S(1)} %get-tuple-element.372), channel_id=1, source_target_pairs={{0,1},{1,0},{2,3},{3,2},{4,5},{5,4},{6,7},{7,6},{8,9},{9,8},{10,11... | collective-permute-start | bytes 1572872 | tf_op jit(solution)/shard_map/ppermute | solution.py:115
  162.7 17.0 %collective-permute-start.36 = (bf16[256,1024]{1,0:T(8,128)(2,1)S(1)}, bf16[256,1024]{1,0:T(8,128)(2,1)S(1)}, u32[]{:S(2)}, u32[]{:S(2)}) collective-permute-start(bf16[256,1024]{1,0:T(8,128)(2,1)S(1)} %get-tuple-element.410), channel_id=1, source_target_pairs={{0,8},{4,12},{8,0},{12,4},{16,24},{20,28},{24,16},{28,20},{1,9},{5... | collective-permute-start | bytes 1572872 | tf_op jit(solution)/shard_map/ppermute | solution.py:115
  166.7 3.8 %collective-permute-start.33 = (bf16[256,1024]{1,0:T(8,128)(2,1)S(1)}, bf16[256,1024]{1,0:T(8,128)(2,1)S(1)}, u32[]{:S(2)}, u32[]{:S(2)}) collective-permute-start(bf16[256,1024]{1,0:T(8,128)(2,1)S(1)} %get-tuple-element.381.refs_0_.refs_5_), channel_id=1, source_target_pairs={{0,1},{1,0},{2,3},{3,2},{4,5},{5,4},{6,7},{7,6},{8,9},{9,8},{10,11... | collective-permute-start | bytes 1572872 | tf_op jit(solution)/shard_map/ppermute | solution.py:115
  167.0 23.2 %collective-permute-start.38 = (bf16[896,512]{1,0:T(8,128)(2,1)S(1)}, bf16[896,512]{1,0:T(8,128)(2,1)S(1)}, u32[]{:S(2)}, u32[]{:S(2)}) collective-permute-start(bf16[896,512]{1,0:T(8,128)(2,1)S(1)} %get-tuple-element.414), channel_id=1, source_target_pairs={{0,2},{1,3},{2,0},{3,1},{4,6},{5,7},{6,4},{7,5},{8,10},{9,11},{10,... | collective-permute-start | bytes 2752520 | tf_op jit(solution)/shard_map/ppermute | solution.py:115
  174.2 5.4 %collective-permute-start.34 = (bf16[256,1024]{1,0:T(8,128)(2,1)S(1)}, bf16[256,1024]{1,0:T(8,128)(2,1)S(1)}, u32[]{:S(2)}, u32[]{:S(2)}) collective-permute-start(bf16[256,1024]{1,0:T(8,128)(2,1)S(1)} %get-tuple-element.397), channel_id=1, source_target_pairs={{0,1},{1,0},{2,3},{3,2},{4,5},{5,4},{6,7},{7,6},{8,9},{9,8},{10,11... | collective-permute-start | bytes 1572872 | tf_op jit(solution)/shard_map/ppermute | solution.py:115
  177.9 34.3 %collective-permute-start.40 = (bf16[512,1024]{1,0:T(8,128)(2,1)S(1)}, bf16[512,1024]{1,0:T(8,128)(2,1)S(1)}, u32[]{:S(2)}, u32[]{:S(2)}) collective-permute-start(bf16[512,1024]{1,0:T(8,128)(2,1)S(1)} %get-tuple-element.421), channel_id=1, source_target_pairs={{0,4},{4,0},{8,12},{12,8},{16,20},{20,16},{24,28},{28,24},{1,5},{5... | collective-permute-start | bytes 3145736 | tf_op jit(solution)/shard_map/ppermute | solution.py:115
  179.9 14.9 %collective-permute-start.37 = (bf16[128,1024]{1,0:T(8,128)(2,1)S(1)}, bf16[128,1024]{1,0:T(8,128)(2,1)S(1)}, u32[]{:S(2)}, u32[]{:S(2)}) collective-permute-start(bf16[128,1024]{1,0:T(8,128)(2,1)S(1)} %get-tuple-element.413), channel_id=1, source_target_pairs={{0,16},{4,20},{8,24},{12,28},{16,0},{20,4},{24,8},{28,12},{1,17},{... | collective-permute-start | bytes 786440 | tf_op jit(solution)/shard_map/ppermute | solution.py:115
  180.9 19.9 %collective-permute-start.35 = (bf16[256,1024]{1,0:T(8,128)(2,1)S(1)}, bf16[256,1024]{1,0:T(8,128)(2,1)S(1)}, u32[]{:S(2)}, u32[]{:S(2)}) collective-permute-start(bf16[256,1024]{1,0:T(8,128)(2,1)S(1)} %get-tuple-element.404), channel_id=1, source_target_pairs={{0,2},{1,3},{2,0},{3,1},{4,6},{5,7},{6,4},{7,5},{8,10},{9,11},{10,... | collective-permute-start | bytes 1572872 | tf_op jit(solution)/shard_map/ppermute | solution.py:115
  186.0 26.0 %collective-permute-start.41 = (bf16[256,1024]{1,0:T(8,128)(2,1)S(1)}, bf16[256,1024]{1,0:T(8,128)(2,1)S(1)}, u32[]{:S(2)}, u32[]{:S(2)}) collective-permute-start(bf16[256,1024]{1,0:T(8,128)(2,1)S(1)} %get-tuple-element.423), channel_id=1, source_target_pairs={{0,8},{4,12},{8,0},{12,4},{16,24},{20,28},{24,16},{28,20},{1,9},{5... | collective-permute-start | bytes 1572872 | tf_op jit(solution)/shard_map/ppermute | solution.py:115
  190.5 49.1 %collective-permute-start.50 = (bf16[896,512]{1,0:T(8,128)(2,1)S(1)}, bf16[896,512]{1,0:T(8,128)(2,1)S(1)}, u32[]{:S(2)}, u32[]{:S(2)}) collective-permute-start(bf16[896,512]{1,0:T(8,128)(2,1)S(1)} %get-tuple-element.441), channel_id=1, source_target_pairs={{0,4},{4,0},{8,12},{12,8},{16,20},{20,16},{24,28},{28,24},{1,5},{5... | collective-permute-start | bytes 2752520 | tf_op jit(solution)/shard_map/ppermute | solution.py:115
  194.9 22.7 %collective-permute-start.44 = (bf16[128,1024]{1,0:T(8,128)(2,1)S(1)}, bf16[128,1024]{1,0:T(8,128)(2,1)S(1)}, u32[]{:S(2)}, u32[]{:S(2)}) collective-permute-start(bf16[128,1024]{1,0:T(8,128)(2,1)S(1)} %get-tuple-element.431.refs_0_), channel_id=1, source_target_pairs={{0,16},{4,20},{8,24},{12,28},{16,0},{20,4},{24,8},{28,12},{1,17},{... | collective-permute-start | bytes 786440 | tf_op jit(solution)/shard_map/ppermute | solution.py:115
  212.1 9.7 %collective-permute-start.43 = (bf16[128,1024]{1,0:T(8,128)(2,1)S(1)}, bf16[128,1024]{1,0:T(8,128)(2,1)S(1)}, u32[]{:S(2)}, u32[]{:S(2)}) collective-permute-start(bf16[128,1024]{1,0:T(8,128)(2,1)S(1)} %get-tuple-element.430), channel_id=1, source_target_pairs={{0,16},{4,20},{8,24},{12,28},{16,0},{20,4},{24,8},{28,12},{1,17},{... | collective-permute-start | bytes 786440 | tf_op jit(solution)/shard_map/ppermute | solution.py:115
  216.2 16.9 %collective-permute-start.42 = (bf16[256,1024]{1,0:T(8,128)(2,1)S(1)}, bf16[256,1024]{1,0:T(8,128)(2,1)S(1)}, u32[]{:S(2)}, u32[]{:S(2)}) collective-permute-start(bf16[256,1024]{1,0:T(8,128)(2,1)S(1)} %get-tuple-element.428), channel_id=1, source_target_pairs={{0,8},{4,12},{8,0},{12,4},{16,24},{20,28},{24,16},{28,20},{1,9},{5... | collective-permute-start | bytes 1572872 | tf_op jit(solution)/shard_map/ppermute | solution.py:115
  216.3 23.4 %collective-permute-start.49 = (bf16[896,512]{1,0:T(8,128)(2,1)S(1)}, bf16[896,512]{1,0:T(8,128)(2,1)S(1)}, u32[]{:S(2)}, u32[]{:S(2)}) collective-permute-start(bf16[896,512]{1,0:T(8,128)(2,1)S(1)} %get-tuple-element.440), channel_id=1, source_target_pairs={{0,2},{1,3},{2,0},{3,1},{4,6},{5,7},{6,4},{7,5},{8,10},{9,11},{10,... | collective-permute-start | bytes 2752520 | tf_op jit(solution)/shard_map/ppermute | solution.py:115
  217.7 37.4 %collective-permute-start.48 = (bf16[256,1024]{1,0:T(8,128)(2,1)S(1)}, bf16[256,1024]{1,0:T(8,128)(2,1)S(1)}, u32[]{:S(2)}, u32[]{:S(2)}) collective-permute-start(bf16[256,1024]{1,0:T(8,128)(2,1)S(1)} %get-tuple-element.439.refs_0_), channel_id=1, source_target_pairs={{0,8},{4,12},{8,0},{12,4},{16,24},{20,28},{24,16},{28,20},{1,9},{5... | collective-permute-start | bytes 1572872 | tf_op jit(solution)/shard_map/ppermute | solution.py:115
  221.8 33.3 %collective-permute-start.46 = (f32[24,1024]{1,0:T(8,128)S(1)}, f32[24,1024]{1,0:T(8,128)S(1)}, u32[]{:S(2)}, u32[]{:S(2)}) collective-permute-start(f32[24,1024]{1,0:T(8,128)S(1)} %get-tuple-element.437.refs_0_), channel_id=1, source_target_pairs={{0,1},{1,0},{2,3},{3,2},{4,5},{5,4},{6,7},{7,6},{8,9},{9,8},{10,11... | collective-permute-start | bytes 294920 | tf_op jit(solution)/shard_map/ppermute | solution.py:115
  233.1 22.0 %collective-permute-start.47 = (bf16[128,1024]{1,0:T(8,128)(2,1)S(1)}, bf16[128,1024]{1,0:T(8,128)(2,1)S(1)}, u32[]{:S(2)}, u32[]{:S(2)}) collective-permute-start(bf16[128,1024]{1,0:T(8,128)(2,1)S(1)} %get-tuple-element.438.refs_0_), channel_id=1, source_target_pairs={{0,16},{4,20},{8,24},{12,28},{16,0},{20,4},{24,8},{28,12},{1,17},{... | collective-permute-start | bytes 786440 | tf_op jit(solution)/shard_map/ppermute | solution.py:115
  239.6 18.2 %collective-permute-start.45 = (bf16[128,1024]{1,0:T(8,128)(2,1)S(1)}, bf16[128,1024]{1,0:T(8,128)(2,1)S(1)}, u32[]{:S(2)}, u32[]{:S(2)}) collective-permute-start(bf16[128,1024]{1,0:T(8,128)(2,1)S(1)} %get-tuple-element.436), channel_id=1, source_target_pairs={{0,16},{4,20},{8,24},{12,28},{16,0},{20,4},{24,8},{28,12},{1,17},{... | collective-permute-start | bytes 786440 | tf_op jit(solution)/shard_map/ppermute | solution.py:115
  240.7 30.3 %collective-permute-start.54 = (bf16[448,512]{1,0:T(8,128)(2,1)S(1)}, bf16[448,512]{1,0:T(8,128)(2,1)S(1)}, u32[]{:S(2)}, u32[]{:S(2)}) collective-permute-start(bf16[448,512]{1,0:T(8,128)(2,1)S(1)} %get-tuple-element.451), channel_id=1, source_target_pairs={{0,8},{4,12},{8,0},{12,4},{16,24},{20,28},{24,16},{28,20},{1,9},{5... | collective-permute-start | bytes 1376264 | tf_op jit(solution)/shard_map/ppermute | solution.py:115
  255.2 19.2 %collective-permute-start.53 = (f32[24,1024]{1,0:T(8,128)S(1)}, f32[24,1024]{1,0:T(8,128)S(1)}, u32[]{:S(2)}, u32[]{:S(2)}) collective-permute-start(f32[24,1024]{1,0:T(8,128)S(1)} %get-tuple-element.449.refs_0_), channel_id=1, source_target_pairs={{0,2},{1,3},{2,0},{3,1},{4,6},{5,7},{6,4},{7,5},{8,10},{9,11},{10,... | collective-permute-start | bytes 294920 | tf_op jit(solution)/shard_map/ppermute | solution.py:115
  255.3 33.3 %collective-permute-start.52 = (bf16[256,1024]{1,0:T(8,128)(2,1)S(1)}, bf16[256,1024]{1,0:T(8,128)(2,1)S(1)}, u32[]{:S(2)}, u32[]{:S(2)}) collective-permute-start(bf16[256,1024]{1,0:T(8,128)(2,1)S(1)} %get-tuple-element.448.refs_0_), channel_id=1, source_target_pairs={{0,8},{4,12},{8,0},{12,4},{16,24},{20,28},{24,16},{28,20},{1,9},{5... | collective-permute-start | bytes 1572872 | tf_op jit(solution)/shard_map/ppermute | solution.py:115
  257.9 30.8 %collective-permute-start.51 = (bf16[128,1024]{1,0:T(8,128)(2,1)S(1)}, bf16[128,1024]{1,0:T(8,128)(2,1)S(1)}, u32[]{:S(2)}, u32[]{:S(2)}) collective-permute-start(bf16[128,1024]{1,0:T(8,128)(2,1)S(1)} %get-tuple-element.447.refs_0_), channel_id=1, source_target_pairs={{0,16},{4,20},{8,24},{12,28},{16,0},{20,4},{24,8},{28,12},{1,17},{... | collective-permute-start | bytes 786440 | tf_op jit(solution)/shard_map/ppermute | solution.py:115
  260.8 30.3 %collective-permute-start.56 = (bf16[512,1024]{1,0:T(8,128)(2,1)S(1)}, bf16[512,1024]{1,0:T(8,128)(2,1)S(1)}, u32[]{:S(2)}, u32[]{:S(2)}) collective-permute-start(bf16[512,1024]{1,0:T(8,128)(2,1)S(1)} %get-tuple-element.457.refs_1_), channel_id=1, source_target_pairs={{0,4},{4,0},{8,12},{12,8},{16,20},{20,16},{24,28},{28,24},{1,5},{5... | collective-permute-start | bytes 3145736 | tf_op jit(solution)/shard_map/ppermute | solution.py:115
  271.2 17.7 %collective-permute-start.58 = (bf16[224,512]{1,0:T(8,128)(2,1)S(1)}, bf16[224,512]{1,0:T(8,128)(2,1)S(1)}, u32[]{:S(2)}, u32[]{:S(2)}) collective-permute-start(bf16[224,512]{1,0:T(8,128)(2,1)S(1)} %get-tuple-element.460), channel_id=1, source_target_pairs={{0,16},{4,20},{8,24},{12,28},{16,0},{20,4},{24,8},{28,12},{1,17},{... | collective-permute-start | bytes 688136 | tf_op jit(solution)/shard_map/ppermute | solution.py:115
  274.5 14.6 %collective-permute-start.57 = (f32[24,1024]{1,0:T(8,128)S(1)}, f32[24,1024]{1,0:T(8,128)S(1)}, u32[]{:S(2)}, u32[]{:S(2)}) collective-permute-start(f32[24,1024]{1,0:T(8,128)S(1)} %get-tuple-element.458.refs_0_), channel_id=1, source_target_pairs={{0,4},{4,0},{8,12},{12,8},{16,20},{20,16},{24,28},{28,24},{1,5},{5... | collective-permute-start | bytes 294920 | tf_op jit(solution)/shard_map/ppermute | solution.py:115
  288.7 14.1 %collective-permute-start.55 = (bf16[256,1024]{1,0:T(8,128)(2,1)S(1)}, bf16[256,1024]{1,0:T(8,128)(2,1)S(1)}, u32[]{:S(2)}, u32[]{:S(2)}) collective-permute-start(bf16[256,1024]{1,0:T(8,128)(2,1)S(1)} %get-tuple-element.456.refs_0_), channel_id=1, source_target_pairs={{0,8},{4,12},{8,0},{12,4},{16,24},{20,28},{24,16},{28,20},{1,9},{5... | collective-permute-start | bytes 1572872 | tf_op jit(solution)/shard_map/ppermute | solution.py:115
  288.8 19.4 %collective-permute-start.64 = (bf16[512,1024]{1,0:T(8,128)(2,1)S(1)}, bf16[512,1024]{1,0:T(8,128)(2,1)S(1)}, u32[]{:S(2)}, u32[]{:S(2)}) collective-permute-start(bf16[512,1024]{1,0:T(8,128)(2,1)S(1)} %get-tuple-element.472.refs_1_), channel_id=1, source_target_pairs={{0,4},{4,0},{8,12},{12,8},{16,20},{20,16},{24,28},{28,24},{1,5},{5... | collective-permute-start | bytes 3145736 | tf_op jit(solution)/shard_map/ppermute | solution.py:115
  288.9 13.9 %collective-permute-start.60 = (bf16[224,512]{1,0:T(8,128)(2,1)S(1)}, bf16[224,512]{1,0:T(8,128)(2,1)S(1)}, u32[]{:S(2)}, u32[]{:S(2)}) collective-permute-start(bf16[224,512]{1,0:T(8,128)(2,1)S(1)} %get-tuple-element.466.refs_0_), channel_id=1, source_target_pairs={{0,16},{4,20},{8,24},{12,28},{16,0},{20,4},{24,8},{28,12},{1,17},{... | collective-permute-start | bytes 688136 | tf_op jit(solution)/shard_map/ppermute | solution.py:115
  289.1 15.9 %collective-permute-start.62 = (f32[24,1024]{1,0:T(8,128)S(1)}, f32[24,1024]{1,0:T(8,128)S(1)}, u32[]{:S(2)}, u32[]{:S(2)}) collective-permute-start(f32[24,1024]{1,0:T(8,128)S(1)} %get-tuple-element.469.refs_0_), channel_id=1, source_target_pairs={{0,8},{4,12},{8,0},{12,4},{16,24},{20,28},{24,16},{28,20},{1,9},{5... | collective-permute-start | bytes 294920 | tf_op jit(solution)/shard_map/ppermute | solution.py:115
  304.9 6.3 %collective-permute-start.63 = (f32[24,1024]{1,0:T(8,128)S(1)}, f32[24,1024]{1,0:T(8,128)S(1)}, u32[]{:S(2)}, u32[]{:S(2)}) collective-permute-start(f32[24,1024]{1,0:T(8,128)S(1)} %get-tuple-element.471.refs_0_.refs_1_), channel_id=1, source_target_pairs={{0,16},{4,20},{8,24},{12,28},{16,0},{20,4},{24,8},{28,12},{1,17},{... | collective-permute-start | bytes 294920 | tf_op jit(solution)/shard_map/ppermute | solution.py:115
  305.0 10.9 %collective-permute-start.61 = (bf16[448,512]{1,0:T(8,128)(2,1)S(1)}, bf16[448,512]{1,0:T(8,128)(2,1)S(1)}, u32[]{:S(2)}, u32[]{:S(2)}) collective-permute-start(bf16[448,512]{1,0:T(8,128)(2,1)S(1)} %get-tuple-element.468.refs_0_), channel_id=1, source_target_pairs={{0,8},{4,12},{8,0},{12,4},{16,24},{20,28},{24,16},{28,20},{1,9},{5... | collective-permute-start | bytes 1376264 | tf_op jit(solution)/shard_map/ppermute | solution.py:115
  305.8 26.1 %collective-permute-start.59 = (bf16[512,1024]{1,0:T(8,128)(2,1)S(1)}, bf16[512,1024]{1,0:T(8,128)(2,1)S(1)}, u32[]{:S(2)}, u32[]{:S(2)}) collective-permute-start(bf16[512,1024]{1,0:T(8,128)(2,1)S(1)} %get-tuple-element.465.refs_1_), channel_id=1, source_target_pairs={{0,4},{4,0},{8,12},{12,8},{16,20},{20,16},{24,28},{28,24},{1,5},{5... | collective-permute-start | bytes 3145736 | tf_op jit(solution)/shard_map/ppermute | solution.py:115
  316.0 33.5 %collective-permute-start.65 = (bf16[896,512]{1,0:T(8,128)(2,1)S(1)}, bf16[896,512]{1,0:T(8,128)(2,1)S(1)}, u32[]{:S(2)}, u32[]{:S(2)}) collective-permute-start(bf16[896,512]{1,0:T(8,128)(2,1)S(1)} %get-tuple-element.487.refs_1_), channel_id=1, source_target_pairs={{0,4},{4,0},{8,12},{12,8},{16,20},{20,16},{24,28},{28,24},{1,5},{5... | collective-permute-start | bytes 2752520 | tf_op jit(solution)/shard_map/ppermute | solution.py:115
  (69 other events, 264.0 us)
where the time goes:
time: 357 us; the launch traced here: 352 us
  waiting for transfers between devices  168 us (47%)
  Pallas kernels  115 us (32%)
  starting transfers between devices  57.3 us (16%)
  local copies, waits for them, and re-layouts  8.9 us (2%)
    ppermute x66, waiting for transfers between devices, swap(): return lax.ppermute(value, axis, [(i, i ^ mask) for i in range(size)])  168 us
    pallas_call x60, Pallas kernels, __call__(): pl.pallas_call(inner, out_shape=outs + [self.token], in_specs=[SMEM] * sm...  86.4 us
    ppermute x66, starting transfers between devices, swap(): return lax.ppermute(value, axis, [(i, i ^ mask) for i in range(size)])  57.3 us
    pallas_call x8, Pallas kernels, __call__(): pl.pallas_call(inner, out_shape=outs + [self.token], grid_spec=pltpu.Pref...  28.2 us
    unnamed x134, local copies, waits for them, and re-layouts  8.89 us
  transfers between devices with their start and end apart: 66, of which 30 were waited for; matrix products, arithmetic and copies ran while one was open for 0% of the time, Pallas kernels for 27%

commit v1 on v0

--- a/solution.py
+++ b/solution.py
@@ -924,19 +924,21 @@
     *saved_a, mixa, part0, part1 = attention(bias_a, 0, x[0], x[1])
     part1 = near(part1)
     vector = jnp.concatenate([dec_qv_bias.reshape(-1), dec_up_bias]).reshape(1, -1)
-    vectors = [vector, chain.pin(near(vector)), far(vector)]
-    both(vectors)
+    vector = chain.pin(vector)
+    vectors = [vector, near(vector), far(vector)]
     part1 = chain.pin(part1)
-    if split:
-        got = chain.pin(got)
-        more = swap(got, "dp", 4)
     both(x)
-    vectors[3] = chain.pin(vectors[3])
+    chain.gap()
     chain.gap()
     *saved_d, mixd, part3 = attention(bias_b, 1, x[3])
     part3 = near(part3)
     *saved_c, mixc, part2 = attention(bias_b, 0, x[2])
+    if split:
+        got = chain.pin(got)
+        more = swap(got, "dp", 4)
     part2 = far(add(part2, part3))
+    vectors[1] = chain.pin(vectors[1])
+    both(vectors)
     packed = pack(jnp.arange(8, dtype=jnp.int32), 8)
     packed_near = near(packed)
     pos, stream = chain(
@@ -957,6 +959,7 @@
     )
     y = [normed2, near(normed2), far(normed2)]
     packed_near = chain.pin(packed_near)
+    vectors[3] = chain.pin(vectors[3])
     if split:
         got = join(got, more)
         more = swap(got, "dp", 1)
@@ -1053,9 +1056,10 @@
     part1 = chain.pin(part1)
     both(g)
     gpc, upc, part2 = feed_back(dgc, g[2])
+    down.product(hbm(hida, hidc, hidd), g)
     gpd, upd, part3 = feed_back(dgd, g[3])
     part3 = near(part3)
-    down.product(hbm(hida, hidc, hidd), g)
+    chain.gap()
     part2 = far(add(part2, part3))
     chain.gap()
     grad_middle, gm_low, sums_mid = chain(
@@ -1066,9 +1070,10 @@
     )
     m = [gm_low, near(gm_low), far(gm_low)]
     up.product(hbm(*y), hbm(gpa, gpc, gpd))
+    down.step()
     g3a, sa, part0, part1 = attention_back(saved_a, m[0], m[1])
     part1 = near(part1)
-    down.step()
+    chain.gap()
     part1 = chain.pin(part1)
     there = far_share(1 - dec.bits[0])
     both(m)
@@ -1076,24 +1081,24 @@
     out_full = chain(out_weight_body, [low(share, width)], (mixa, mixc, mixd, *m))[0]
     g3d, sd, part3 = attention_back(saved_d, m[3])
     part3 = near(part3)
+    down.step()
     attn.product(hbm(*x), hbm(g3a, g3c, g3d), [out_full])
     part2 = far(add(part2, part3))
+    up.step()
     down.step()
     up.step()
-    dec.shares(kept_share, sent, there)
-    down.step()
     grad_tokens, sums = chain(
         last_body,
         [kept(full(n, width)), full(24, width)],
         (at, grad_middle, part0, part1, part2, stream, enc_gain, sa, sc, sd, sums_mid),
         smem=1,
     )
+    dec.shares(kept_share, sent, there)
     dec.other(far_share(dec.bits[0]))
+    down.step()
+    attn.step()
     up.step()
-    attn.step()
     down.step()
-    up.step()
-    attn.step()
     dec.step()
     hops = [("mp", 1), ("mp", 2)] + [("dp", 1 << i) for i in range(dec.size.bit_length() - 1)]
     hops = iter(hops)
@@ -1106,21 +1111,21 @@
         return total, None
 
     small = hop(sums)
-    down.step()
+    attn.step()
     up.step()
+    small = hop(*small)
+    dec.step()
+    attn.step()
+    up.step()
+    e_down = finish((down,), [(ff, width)], [(0, 0, None, 0, ff // 8, 0, ff // 8, 0, width, 0)])[0]
     small = hop(*small)
     attn.step()
     dec.step()
     small = hop(*small)
-    up.step()
     attn.step()
+    e_up = finish((up,), [(width, ff)], [(0, 0, None, 0, width // 8, 0, width // 8, 0, ff, 0)])[0]
     dec.step()
     small = hop(*small)
-    e_down = finish((down,), [(ff, width)], [(0, 0, None, 0, ff // 8, 0, ff // 8, 0, width, 0)])[0]
-    attn.step()
-    dec.step()
-    small = hop(*small)
-    e_up = finish((up,), [(width, ff)], [(0, 0, None, 0, width // 8, 0, width // 8, 0, ff, 0)])[0]
     while small[1] is not None:
         sums = small
         small = hop(*small)

time: 357 us -> 361 us (1.011)
  waiting for transfers between devices: 168 us -> 177 us
    ppermute x66, waiting for transfers between devices: 168 us -> 177 us  [swap(): return lax.ppermute(value, axis, [(i, i ^ mask) for i in range(size)])]
    unnamed x134 -> x142, local copies, waits for them, and re-layouts: 8.89 us -> 6.6 us
    pallas_call x60 -> x63, Pallas kernels: 86.4 us -> 86.7 us  [__call__(): pl.pallas_call(inner, out_shape=outs + [self.token], in_specs=[SMEM] * sm...]
  transfers between devices with their start and end apart: 66 -> 66, of which waited for: 30 -> 32; matrix products, arithmetic and copies ran while one was open for 0% -> 0% of each run, Pallas kernels for 27% -> 26%
where the time goes in v1:
time: 361 us; the launch traced here: 354 us
  waiting for transfers between devices  177 us (49%)
  Pallas kernels  114 us (32%)
  starting transfers between devices  53.8 us (15%)
  local copies, waits for them, and re-layouts  6.6 us (2%)
    ppermute x66, waiting for transfers between devices, swap(): return lax.ppermute(value, axis, [(i, i ^ mask) for i in range(size)])  177 us
    pallas_call x63, Pallas kernels, __call__(): pl.pallas_call(inner, out_shape=outs + [self.token], in_specs=[SMEM] * sm...  86.7 us
    ppermute x66, starting transfers between devices, swap(): return lax.ppermute(value, axis, [(i, i ^ mask) for i in range(size)])  53.8 us
    pallas_call x8, Pallas kernels, __call__(): pl.pallas_call(inner, out_shape=outs + [self.token], grid_spec=pltpu.Pref...  27.7 us
  transfers between devices with their start and end apart: 66, of which 32 were waited for; matrix products, arithmetic and copies ran while one was open for 0% of the time, Pallas kernels for 26%

profile of v1, /device:TPU:0, one launch (start us, length us, event | category | flops | bytes accessed | tf_op | source)
XLA Modules:
  0.0 353.6 jit_solution(11815750797410052058)
XLA Ops:
  1.6 2.4 shard_map.400
  4.6 2.6 collective-permute-start.3
  7.3 1.9 shard_map.401
  10.9 4.4 %shard_map.402 = (bf16[2,256,256]{2,1,0:T(8,128)(2,1)}, bf16[2,256,256]{2,1,0:T(8,128)(2,1)}, bf16[2,256,256]{2,1,0:T(8,128)(2,1)}, bf16[2,4,256,256]{3,2,1,0:T(...) custom-call(bf16[256,1024]{1,0:T(8,128)(2,1)S(1)} %get-tuple-element, ...), custom_call_target="tpu_custom_call" | custom-call | flops 10000000000 | bytes 100000000 | tf_op jit(solution)/shard_map/pallas_call | solution.py:56
  15.8 1.9 collective-permute-start.1
  17.7 2.4 collective-permute-done.3.value_ref
  20.1 2.1 collective-permute-done.5.refs_0_.refs_4_
  22.2 2.4 shard_map.408
  24.6 3.5 shard_map.409
  28.2 3.0 collective-permute-start.9
  33.6 4.7 %shard_map.414 = (bf16[1792,512]{1,0:T(8,128)(2,1)S(1)}, f32[8,128]{1,0:T(8,128)S(1)}) custom-call(s32[8]{0:T(128)S(1)} %iota.16.refs_0_, bf16[512,512]{1,0:T(8,128)(2,1)} %refs_1_.10, bf16[512,512]{1,0:T(8,128)(2,1)} %refs_2_.13, bf16[128,512]{1,0:T(8,128)(2,1)} %refs_3_.17, bf16[3,512,128]{2,1,0:T(8,128)(2,1)} %refs_4_.14, bf16[1024,128]{1,0:T(8,128)(2,1)} %refs_5_.11, ...), custom_call_target="tpu_custom_call" | custom-call | flops 10000000000 | bytes 100000000 | tf_op jit(solution)/shard_map/pallas_call | solution.py:66
  38.9 3.3 shard_map.415
  48.2 8.0 %collective-permute-done.11.refs_1_ = bf16[448,512]{1,0:T(8,128)(2,1)S(1)} collective-permute-done((bf16[448,512]{1,0:T(8,128)(2,1)S(1)}, bf16[448,512]{1,0:T(8,128)(2,1)S(1)}, u32[]{:S(2)}, u32[]{:S(2)}) %collective-permute-start.11) | collective-permute-done | bytes 458784 | tf_op jit(solution)/shard_map/ppermute | solution.py:115
  58.4 4.3 %shard_map.421 = (bf16[2,256,1024]{2,1,0:T(8,128)(2,1)}, bf16[2,256,1024]{2,1,0:T(8,128)(2,1)}, bf16[256,1024]{1,0:T(8,128)(2,1)S(1)}, bf16[256,1024]{1,0:T(8,128)(2,1)S(1)}, f32[8,128]{1,0:T(8,128)S(1)}) custom-call(bf16[256,1024]{1,0:T(8,128)(2,1)S(1)} %get-tuple-element.294.refs_0_.refs_1_, bf16[256,1024]{1,0:T(8,128)(2,1)S(1)} %collective-permute-done.10.refs_1_.refs_2_, ...), custom_call_target="tpu_custom_call" | custom-call | flops 10000000000 | bytes 100000000 | tf_op jit(solution)/shard_map/pallas_call | solution.py:56
  65.4 2.5 shard_map.425
  68.0 2.5 shard_map.426
  71.7 7.4 %collective-permute-done.20.value_ref = bf16[896,512]{1,0:T(8,128)(2,1)S(1)} collective-permute-done((bf16[896,512]{1,0:T(8,128)(2,1)S(1)}, bf16[896,512]{1,0:T(8,128)(2,1)S(1)}, u32[]{:S(2)}, u32[]{:S(2)}) %collective-permute-start.20) | collective-permute-done | bytes 917536 | tf_op jit(solution)/shard_map/ppermute | solution.py:115
  79.1 5.8 %collective-permute-done.19.value_ref = bf16[256,1024]{1,0:T(8,128)(2,1)S(1)} collective-permute-done((bf16[256,1024]{1,0:T(8,128)(2,1)S(1)}, bf16[256,1024]{1,0:T(8,128)(2,1)S(1)}, u32[]{:S(2)}, u32[]{:S(2)}) %collective-permute-start.19) | collective-permute-done | bytes 524320 | tf_op jit(solution)/shard_map/ppermute | solution.py:115
  86.6 17.5 %shard_map.430 = (bf16[256,1024]{1,0:T(8,128)(2,1)}, f32[256,512]{1,0:T(8,128)}, bf16[256,512]{1,0:T(8,128)(2,1)}, bf16[256,512]{1,0:T(8,128)(2,1)}, bf16[256,20...) custom-call(s32[2]{0:T(128)S(1)} %pad_add_fusion.refs_0_, ...), custom_call_target="tpu_custom_call" | custom-call | flops 10000000000 | bytes 100000000 | tf_op jit(solution)/shard_map/pallas_call | solution.py:56
  106.4 3.1 shard_map.432
  109.8 4.4 %shard_map.433 = (bf16[2,1792,512]{2,1,0:T(8,128)(2,1)S(1)}, bf16[2,1792,512]{2,1,0:T(8,128)(2,1)}, f32[8,128]{1,0:T(8,128)S(1)}) custom-call(bf16[256,512]{1,0:T(8,128)(2,1)S(1)} %copy-done.44, bf16[256,512]{1,0:T(8,128)(2,1)S(1)} %copy-done.45, bf16[256,2048]{1,0:T(8,128)(2,1)S(1)} %copy-done.27, bf16[256,512]{1,0:T(8,128)(2,1)S(1)} %copy-done.46, ...), custom_call_target="tpu_custom_call" | custom-call | flops 10000000000 | bytes 100000000 | tf_op jit(solution)/shard_map/pallas_call | solution.py:56
  114.5 3.9 %collective-permute-done.24.value_ref = bf16[256,1024]{1,0:T(8,128)(2,1)S(1)} collective-permute-done((bf16[256,1024]{1,0:T(8,128)(2,1)S(1)}, bf16[256,1024]{1,0:T(8,128)(2,1)S(1)}, u32[]{:S(2)}, u32[]{:S(2)}) %collective-permute-start.24) | collective-permute-done | bytes 524320 | tf_op jit(solution)/shard_map/ppermute | solution.py:115
  119.5 1.9 shard_map.436
  121.4 3.2 shard_map.437
  124.5 1.9 shard_map.438
  129.7 13.0 %collective-permute-done.27.refs_4_ = bf16[256,1024]{1,0:T(8,128)(2,1)S(1)} collective-permute-done((bf16[256,1024]{1,0:T(8,128)(2,1)S(1)}, bf16[256,1024]{1,0:T(8,128)(2,1)S(1)}, u32[]{:S(2)}, u32[]{:S(2)}) %collective-permute-start.27) | collective-permute-done | bytes 524320 | tf_op jit(solution)/shard_map/ppermute | solution.py:115
  142.7 2.0 shard_map.442
  145.8 3.9 %shard_map.443 = (bf16[512,1024]{1,0:T(8,128)(2,1)S(1)}, f32[8,128]{1,0:T(8,128)S(1)}) custom-call(s32[2]{0:T(128)S(1)} %pad_add_fusion.1.refs_0_, bf16[256,1024]{1,0:T(8,128)(2,1)} %copy-done.7, bf16[256,1024]{1,0:T(8,128)(2,1)} %copy-done.8, bf16[256,1024]{1,0:T(8,128)(2,1)} %copy-done.10, bf16[256,1024]{1,0:T(8,128)(2,1)} %copy-done.9, ...), custom_call_target="tpu_custom_call" | custom-call | flops 10000000000 | bytes 100000000 | tf_op jit(solution)/shard_map/pallas_call | solution.py:66
  149.7 2.3 collective-permute-done.29.refs_8_
  152.0 3.4 shard_map.444
  157.0 1.7 collective-permute-start.37
  158.8 4.7 %shard_map.445 = (bf16[2,256,768]{2,1,0:T(8,128)(2,1)}, f32[2,256]{1,0:T(2,128)}, bf16[256,1024]{1,0:T(8,128)(2,1)S(1)}, bf16[256,1024]{1,0:T(8,128)(2,1)S(1)}, f32[8,128]{1,0:T(8,128)S(1)}) custom-call(bf16[256,1024]{1,0:T(8,128)(2,1)S(1)} %get-tuple-element.365.refs_0_.refs_3_, bf16[256,1024]{1,0:T(8,128)(2,1)S(1)} %collective-permute-done.28.refs_1_.refs_4_, ...), custom_call_target="tpu_custom_call" | custom-call | flops 10000000000 | bytes 100000000 | tf_op jit(solution)/shard_map/pallas_call | solution.py:56
  163.5 1.9 collective-permute-done.30.value_ref
  167.5 2.6 shard_map.450
  171.2 2.6 shard_map.452
  173.9 3.0 collective-permute-start.39
  177.0 3.5 %shard_map.454 = (bf16[512,1024]{1,0:T(8,128)(2,1)S(1)}, f32[8,128]{1,0:T(8,128)S(1)}) custom-call(s32[2]{0:T(128)S(1)} %pad_add_fusion.1.refs_0_, bf16[256,1024]{1,0:T(8,128)(2,1)} %copy-done.4, bf16[256,1024]{1,0:T(8,128)(2,1)} %copy-done.5, bf16[256,1024]{1,0:T(8,128)(2,1)} %get-tuple-element.273.refs_0_.refs_3_, bf16[256,1024]{1,0:T(8,128)(2,1)} %copy-done.6, ...), custom_call_target="tpu_custom_call" | custom-call | flops 10000000000 | bytes 100000000 | tf_op jit(solution)/shard_map/pallas_call | solution.py:66
  181.4 4.0 %shard_map.456 = (bf16[256,1024]{1,0:T(8,128)(2,1)S(1)}, bf16[256,1024]{1,0:T(8,128)(2,1)S(1)}, f32[8,128]{1,0:T(8,128)S(1)}) custom-call(s32[4]{0:T(128)S(1)} %pad_add_fusion.2.refs_0_, bf16[256,1024]{1,0:T(8,128)(2,1)} %copy-done.7, bf16[256,1024]{1,0:T(8,128)(2,1)} %copy-done.8, bf16[256,1024]{1,0:T(8,128)(2,1)} %copy-done.10, ...), custom_call_target="tpu_custom_call" | custom-call | flops 10000000000 | bytes 100000000 | tf_op jit(solution)/shard_map/pallas_call | solution.py:66
  186.8 2.5 collective-permute-done.39.refs_1_
  190.9 15.2 %collective-permute-done.38.refs_2_ = bf16[256,1024]{1,0:T(8,128)(2,1)S(1)} collective-permute-done((bf16[256,1024]{1,0:T(8,128)(2,1)S(1)}, bf16[256,1024]{1,0:T(8,128)(2,1)S(1)}, u32[]{:S(2)}, u32[]{:S(2)}) %collective-permute-start.38) | collective-permute-done | bytes 524320 | tf_op jit(solution)/shard_map/ppermute | solution.py:115
  207.6 1.9 shard_map.459
  210.2 2.0 collective-permute-start.46
  213.7 3.9 %shard_map.463 = (bf16[256,1024]{1,0:T(8,128)(2,1)S(1)}, bf16[256,1024]{1,0:T(8,128)(2,1)S(1)}, f32[8,128]{1,0:T(8,128)S(1)}) custom-call(s32[4]{0:T(128)S(1)} %pad_add_fusion.2.refs_0_, bf16[256,1024]{1,0:T(8,128)(2,1)} %copy-done.4, bf16[256,1024]{1,0:T(8,128)(2,1)} %copy-done.5, bf16[256,1024]{1,0:T(8,128)(2,1)} %get-tuple-element.273.refs_0_.refs_3_, ...), custom_call_target="tpu_custom_call" | custom-call | flops 10000000000 | bytes 100000000 | tf_op jit(solution)/shard_map/pallas_call | solution.py:66
  217.7 2.6 collective-permute-done.47.refs_1_
  220.4 10.2 %collective-permute-done.46.refs_1_ = bf16[256,1024]{1,0:T(8,128)(2,1)S(1)} collective-permute-done((bf16[256,1024]{1,0:T(8,128)(2,1)S(1)}, bf16[256,1024]{1,0:T(8,128)(2,1)S(1)}, u32[]{:S(2)}, u32[]{:S(2)}) %collective-permute-start.46) | collective-permute-done | bytes 524320 | tf_op jit(solution)/shard_map/ppermute | solution.py:115
  231.1 2.0 collective-permute-done.44.refs_3_
  236.7 10.8 %collective-permute-done.43.refs_2_ = bf16[256,1024]{1,0:T(8,128)(2,1)S(1)} collective-permute-done((bf16[256,1024]{1,0:T(8,128)(2,1)S(1)}, bf16[256,1024]{1,0:T(8,128)(2,1)S(1)}, u32[]{:S(2)}, u32[]{:S(2)}) %collective-permute-start.43) | collective-permute-done | bytes 524320 | tf_op jit(solution)/shard_map/ppermute | solution.py:115
  248.1 2.5 collective-permute-start.55
  251.9 11.1 %collective-permute-done.49.refs_2_ = bf16[448,512]{1,0:T(8,128)(2,1)S(1)} collective-permute-done((bf16[448,512]{1,0:T(8,128)(2,1)S(1)}, bf16[448,512]{1,0:T(8,128)(2,1)S(1)}, u32[]{:S(2)}, u32[]{:S(2)}) %collective-permute-start.49) | collective-permute-done | bytes 458784 | tf_op jit(solution)/shard_map/ppermute | solution.py:115
  263.6 2.5 collective-permute-start.58
  266.1 11.8 %collective-permute-done.55.refs_1_ = bf16[256,1024]{1,0:T(8,128)(2,1)S(1)} collective-permute-done((bf16[256,1024]{1,0:T(8,128)(2,1)S(1)}, bf16[256,1024]{1,0:T(8,128)(2,1)S(1)}, u32[]{:S(2)}, u32[]{:S(2)}) %collective-permute-start.55) | collective-permute-done | bytes 524320 | tf_op jit(solution)/shard_map/ppermute | solution.py:115
  278.0 2.3 shard_map.473
  280.3 2.1 collective-permute-start.57
  283.7 2.4 collective-permute-done.58.refs_1_
  286.3 18.1 %collective-permute-done.57.refs_1_ = f32[24,1024]{1,0:T(8,128)S(1)} collective-permute-done((f32[24,1024]{1,0:T(8,128)S(1)}, f32[24,1024]{1,0:T(8,128)S(1)}, u32[]{:S(2)}, u32[]{:S(2)}) %collective-permute-start.57) | collective-permute-done | bytes 98336 | tf_op jit(solution)/shard_map/ppermute | solution.py:115
  304.5 2.3 shard_map.479
  306.9 2.2 collective-permute-done.63.refs_1_
  309.9 2.0 collective-permute-start.62
  311.9 3.6 %collective-permute-done.64.refs_1_.refs_2_ = f32[24,1024]{1,0:T(8,128)S(1)} collective-permute-done((f32[24,1024]{1,0:T(8,128)S(1)}, f32[24,1024]{1,0:T(8,128)S(1)}, u32[]{:S(2)}, u32[]{:S(2)}) %collective-permute-start.64) | collective-permute-done | bytes 98336 | tf_op jit(solution)/shard_map/ppermute | solution.py:115
  316.8 4.6 %collective-permute-done.62.refs_1_ = bf16[448,512]{1,0:T(8,128)(2,1)S(1)} collective-permute-done((bf16[448,512]{1,0:T(8,128)(2,1)S(1)}, bf16[448,512]{1,0:T(8,128)(2,1)S(1)}, u32[]{:S(2)}, u32[]{:S(2)}) %collective-permute-start.62) | collective-permute-done | bytes 458784 | tf_op jit(solution)/shard_map/ppermute | solution.py:115
  322.8 12.9 %collective-permute-done.59.refs_2_ = bf16[512,1024]{1,0:T(8,128)(2,1)S(1)} collective-permute-done((bf16[512,1024]{1,0:T(8,128)(2,1)S(1)}, bf16[512,1024]{1,0:T(8,128)(2,1)S(1)}, u32[]{:S(2)}, u32[]{:S(2)}) %collective-permute-start.59) | collective-permute-done | bytes 1048608 | tf_op jit(solution)/shard_map/ppermute | solution.py:115
  335.7 2.3 shard_map.485
  338.0 13.4 %collective-permute-done.65.refs_2_ = bf16[896,512]{1,0:T(8,128)(2,1)S(1)} collective-permute-done((bf16[896,512]{1,0:T(8,128)(2,1)S(1)}, bf16[896,512]{1,0:T(8,128)(2,1)S(1)}, u32[]{:S(2)}, u32[]{:S(2)}) %collective-permute-start.65) | collective-permute-done | bytes 917536 | tf_op jit(solution)/shard_map/ppermute | solution.py:115
  351.3 2.1 shard_map.486
  (307 shorter events, 52.9 us)
Async XLA Ops:
  4.1 5.5 %collective-permute-start = (bf16[256,1024]{1,0:T(8,128)(2,1)S(1)}, bf16[256,1024]{1,0:T(8,128)(2,1)S(1)}, u32[]{:S(2)}, u32[]{:S(2)}) collective-permute-start(bf16[256,1024]{1,0:T(8,128)(2,1)S(1)} %get-tuple-element.264.refs_0_.refs_1_), channel_id=1, source_target_pairs={{0,1},{1,0},{2,3},{3,2},{4,5},{5,4},{6,7},{7,6},{8,9},{9,8},{10,11... | collective-permute-start | bytes 1572872 | tf_op jit(solution)/shard_map/ppermute | solution.py:115
  4.6 15.5 %collective-permute-start.3 = (bf16[256,1024]{1,0:T(8,128)(2,1)S(1)}, bf16[256,1024]{1,0:T(8,128)(2,1)}, u32[]{:S(2)}, u32[]{:S(2)}) collective-permute-start(bf16[256,1024]{1,0:T(8,128)(2,1)S(1)} %get-tuple-element.264.refs_0_.refs_1_), channel_id=1, source_target_pairs={{0,2},{1,3},{2,0},{3,1},{4,6},{5,7},{6,4},{7,5},{8,10},{9,11},{10,... | collective-permute-start | bytes 1572872 | tf_op jit(solution)/shard_map/ppermute | solution.py:115
  7.2 21.1 %collective-permute-start.7 = (bf16[224,512]{1,0:T(8,128)(2,1)S(1)}, bf16[224,512]{1,0:T(8,128)(2,1)}, u32[]{:S(2)}, u32[]{:S(2)}) collective-permute-start(bf16[224,512]{1,0:T(8,128)(2,1)S(1)} %get-tuple-element.279), channel_id=1, source_target_pairs={{0,2},{1,3},{2,0},{3,1},{4,6},{5,7},{6,4},{7,5},{8,10},{9,11},{10,... | collective-permute-start | bytes 688136 | tf_op jit(solution)/shard_map/ppermute | solution.py:115
  15.2 2.4 collective-permute-start.4
  15.3 17.7 %collective-permute-start.2 = (f32[1,768]{1,0:T(1,128)S(1)}, f32[1,768]{1,0:T(1,128)S(1)}, u32[]{:S(2)}, u32[]{:S(2)}) collective-permute-start(f32[1,768]{1,0:T(1,128)S(1)} %get-tuple-element.269.refs_12_), channel_id=1, source_target_pairs={{0,1},{1,0},{2,3},{3,2},{4,5},{5,4},{6,7},{7,6},{8,9},{9,8},{10,11... | collective-permute-start | bytes 9224 | tf_op jit(solution)/shard_map/ppermute | solution.py:115
  15.8 17.3 %collective-permute-start.1 = (f32[1,768]{1,0:T(1,128)S(1)}, f32[1,768]{1,0:T(1,128)S(1)}, u32[]{:S(2)}, u32[]{:S(2)}) collective-permute-start(f32[1,768]{1,0:T(1,128)S(1)} %get-tuple-element.269.refs_12_), channel_id=1, source_target_pairs={{0,2},{1,3},{2,0},{3,1},{4,6},{5,7},{6,4},{7,5},{8,10},{9,11},{10,... | collective-permute-start | bytes 9224 | tf_op jit(solution)/shard_map/ppermute | solution.py:115
  20.1 2.1 collective-permute-start.5
  28.1 3.2 collective-permute-start.6
  28.2 14.3 %collective-permute-start.9 = (bf16[224,512]{1,0:T(8,128)(2,1)}, bf16[224,512]{1,0:T(8,128)(2,1)S(1)}, u32[]{:S(2)}, u32[]{:S(2)}) collective-permute-start(bf16[224,512]{1,0:T(8,128)(2,1)} %get-tuple-element.290.refs_0_), channel_id=1, source_target_pairs={{0,16},{4,20},{8,24},{12,28},{16,0},{20,4},{24,8},{28,12},{1,17},{... | collective-permute-start | bytes 688136 | tf_op jit(solution)/shard_map/ppermute | solution.py:115
  31.4 14.0 %collective-permute-start.8 = (bf16[256,1024]{1,0:T(8,128)(2,1)S(1)}, bf16[256,1024]{1,0:T(8,128)(2,1)S(1)}, u32[]{:S(2)}, u32[]{:S(2)}) collective-permute-start(bf16[256,1024]{1,0:T(8,128)(2,1)S(1)} %get-tuple-element.289), channel_id=1, source_target_pairs={{0,2},{1,3},{2,0},{3,1},{4,6},{5,7},{6,4},{7,5},{8,10},{9,11},{10,... | collective-permute-start | bytes 1572872 | tf_op jit(solution)/shard_map/ppermute | solution.py:115
  38.3 9.9 %collective-permute-start.13 = (bf16[1792,512]{1,0:T(8,128)(2,1)S(1)}, bf16[1792,512]{1,0:T(8,128)(2,1)S(1)}, u32[]{:S(2)}, u32[]{:S(2)}) collective-permute-start(bf16[1792,512]{1,0:T(8,128)(2,1)S(1)} %get-tuple-element.297.refs_6_), channel_id=1, source_target_pairs={{0,1},{1,0},{2,3},{3,2},{4,5},{5,4},{6,7},{7,6},{8,9},{9,8},{10,11... | collective-permute-start | bytes 5505032 | tf_op jit(solution)/shard_map/ppermute | solution.py:115
  38.4 9.8 %collective-permute-start.12 = (f32[1,768]{1,0:T(1,128)S(1)}, f32[1,768]{1,0:T(1,128)S(1)}, u32[]{:S(2)}, u32[]{:S(2)}) collective-permute-start(f32[1,768]{1,0:T(1,128)S(1)} %get-tuple-element.296.refs_14_), channel_id=1, source_target_pairs={{0,1},{1,0},{2,3},{3,2},{4,5},{5,4},{6,7},{7,6},{8,9},{9,8},{10,11... | collective-permute-start | bytes 9224 | tf_op jit(solution)/shard_map/ppermute | solution.py:115
  43.6 12.6 %collective-permute-start.11 = (bf16[448,512]{1,0:T(8,128)(2,1)S(1)}, bf16[448,512]{1,0:T(8,128)(2,1)S(1)}, u32[]{:S(2)}, u32[]{:S(2)}) collective-permute-start(bf16[448,512]{1,0:T(8,128)(2,1)S(1)} %get-tuple-element.295.refs_0_), channel_id=1, source_target_pairs={{0,8},{4,12},{8,0},{12,4},{16,24},{20,28},{24,16},{28,20},{1,9},{5... | collective-permute-start | bytes 1376264 | tf_op jit(solution)/shard_map/ppermute | solution.py:115
  46.7 11.2 %collective-permute-start.10 = (bf16[256,1024]{1,0:T(8,128)(2,1)S(1)}, bf16[256,1024]{1,0:T(8,128)(2,1)S(1)}, u32[]{:S(2)}, u32[]{:S(2)}) collective-permute-start(bf16[256,1024]{1,0:T(8,128)(2,1)S(1)} %get-tuple-element.294.refs_0_.refs_1_), channel_id=1, source_target_pairs={{0,1},{1,0},{2,3},{3,2},{4,5},{5,4},{6,7},{7,6},{8,9},{9,8},{10,11... | collective-permute-start | bytes 1572872 | tf_op jit(solution)/shard_map/ppermute | solution.py:115
  46.7 16.1 %collective-permute-start.15 = (bf16[256,1024]{1,0:T(8,128)(2,1)S(1)}, bf16[256,1024]{1,0:T(8,128)(2,1)S(1)}, u32[]{:S(2)}, u32[]{:S(2)}) collective-permute-start(bf16[256,1024]{1,0:T(8,128)(2,1)S(1)} %get-tuple-element.294.refs_0_.refs_1_), channel_id=1, source_target_pairs={{0,2},{1,3},{2,0},{3,1},{4,6},{5,7},{6,4},{7,5},{8,10},{9,11},{10,... | collective-permute-start | bytes 1572872 | tf_op jit(solution)/shard_map/ppermute | solution.py:115
  56.3 8.4 %collective-permute-start.17 = (bf16[896,512]{1,0:T(8,128)(2,1)S(1)}, bf16[896,512]{1,0:T(8,128)(2,1)S(1)}, u32[]{:S(2)}, u32[]{:S(2)}) collective-permute-start(bf16[896,512]{1,0:T(8,128)(2,1)S(1)} %get-tuple-element.308.refs_8_), channel_id=1, source_target_pairs={{0,1},{1,0},{2,3},{3,2},{4,5},{5,4},{6,7},{7,6},{8,9},{9,8},{10,11... | collective-permute-start | bytes 2752520 | tf_op jit(solution)/shard_map/ppermute | solution.py:115
  56.3 22.8 %collective-permute-start.20 = (bf16[896,512]{1,0:T(8,128)(2,1)S(1)}, bf16[896,512]{1,0:T(8,128)(2,1)S(1)}, u32[]{:S(2)}, u32[]{:S(2)}) collective-permute-start(bf16[896,512]{1,0:T(8,128)(2,1)S(1)} %get-tuple-element.308.refs_8_), channel_id=1, source_target_pairs={{0,4},{4,0},{8,12},{12,8},{16,20},{20,16},{24,28},{28,24},{1,5},{5... | collective-permute-start | bytes 2752520 | tf_op jit(solution)/shard_map/ppermute | solution.py:115
  62.7 1.9 collective-permute-start.14
  62.8 2.6 collective-permute-start.16
  67.9 2.6 collective-permute-start.18
  70.6 14.3 %collective-permute-start.19 = (bf16[256,1024]{1,0:T(8,128)(2,1)S(1)}, bf16[256,1024]{1,0:T(8,128)(2,1)S(1)}, u32[]{:S(2)}, u32[]{:S(2)}) collective-permute-start(bf16[256,1024]{1,0:T(8,128)(2,1)S(1)} %get-tuple-element.315), channel_id=1, source_target_pairs={{0,2},{1,3},{2,0},{3,1},{4,6},{5,7},{6,4},{7,5},{8,10},{9,11},{10,... | collective-permute-start | bytes 1572872 | tf_op jit(solution)/shard_map/ppermute | solution.py:115
  79.1 5.9 %collective-permute-start.21 = (bf16[896,512]{1,0:T(8,128)(2,1)S(1)}, bf16[896,512]{1,0:T(8,128)(2,1)S(1)}, u32[]{:S(2)}, u32[]{:S(2)}) collective-permute-start(bf16[896,512]{1,0:T(8,128)(2,1)S(1)} %get-tuple-element.320.refs_9_), channel_id=1, source_target_pairs={{0,1},{1,0},{2,3},{3,2},{4,5},{5,4},{6,7},{7,6},{8,9},{9,8},{10,11... | collective-permute-start | bytes 2752520 | tf_op jit(solution)/shard_map/ppermute | solution.py:115
  104.1 14.3 %collective-permute-start.24 = (bf16[256,1024]{1,0:T(8,128)(2,1)S(1)}, bf16[256,1024]{1,0:T(8,128)(2,1)S(1)}, u32[]{:S(2)}, u32[]{:S(2)}) collective-permute-start(bf16[256,1024]{1,0:T(8,128)(2,1)S(1)} %get-tuple-element.328.refs_0_.refs_4_), channel_id=1, source_target_pairs={{0,2},{1,3},{2,0},{3,1},{4,6},{5,7},{6,4},{7,5},{8,10},{9,11},{10,... | collective-permute-start | bytes 1572872 | tf_op jit(solution)/shard_map/ppermute | solution.py:115
  109.6 5.0 %collective-permute-start.23 = (bf16[256,1024]{1,0:T(8,128)(2,1)S(1)}, bf16[256,1024]{1,0:T(8,128)(2,1)S(1)}, u32[]{:S(2)}, u32[]{:S(2)}) collective-permute-start(bf16[256,1024]{1,0:T(8,128)(2,1)S(1)} %get-tuple-element.332), channel_id=1, source_target_pairs={{0,1},{1,0},{2,3},{3,2},{4,5},{5,4},{6,7},{7,6},{8,9},{9,8},{10,11... | collective-permute-start | bytes 1572872 | tf_op jit(solution)/shard_map/ppermute | solution.py:115
  114.2 51.2 %collective-permute-start.32 = (bf16[2,1792,512]{2,1,0:T(8,128)(2,1)S(1)}, bf16[2,1792,512]{2,1,0:T(8,128)(2,1)S(1)}, u32[]{:S(2)}, u32[]{:S(2)}) collective-permute-start(bf16[2,1792,512]{2,1,0:T(8,128)(2,1)S(1)} %get-tuple-element.382), channel_id=1, source_target_pairs={{0,1},{1,0},{2,3},{3,2},{4,5},{5,4},{6,7},{7,6},{8,9},{9,8},{10,11... | collective-permute-start | bytes 11010056 | tf_op jit(solution)/shard_map/ppermute | solution.py:115
  118.4 2.9 collective-permute-start.25
  126.4 2.0 collective-permute-start.26
  126.8 25.2 %collective-permute-start.29 = (bf16[512,1024]{1,0:T(8,128)(2,1)S(1)}, bf16[512,1024]{1,0:T(8,128)(2,1)S(1)}, u32[]{:S(2)}, u32[]{:S(2)}) collective-permute-start(bf16[512,1024]{1,0:T(8,128)(2,1)S(1)} %get-tuple-element.370), channel_id=1, source_target_pairs={{0,4},{4,0},{8,12},{12,8},{16,20},{20,16},{24,28},{28,24},{1,5},{5... | collective-permute-start | bytes 3145736 | tf_op jit(solution)/shard_map/ppermute | solution.py:115
  128.6 14.1 %collective-permute-start.27 = (bf16[256,1024]{1,0:T(8,128)(2,1)S(1)}, bf16[256,1024]{1,0:T(8,128)(2,1)S(1)}, u32[]{:S(2)}, u32[]{:S(2)}) collective-permute-start(bf16[256,1024]{1,0:T(8,128)(2,1)S(1)} %get-tuple-element.358), channel_id=1, source_target_pairs={{0,2},{1,3},{2,0},{3,1},{4,6},{5,7},{6,4},{7,5},{8,10},{9,11},{10,... | collective-permute-start | bytes 1572872 | tf_op jit(solution)/shard_map/ppermute | solution.py:115
  144.7 14.0 %collective-permute-start.28 = (bf16[256,1024]{1,0:T(8,128)(2,1)S(1)}, bf16[256,1024]{1,0:T(8,128)(2,1)S(1)}, u32[]{:S(2)}, u32[]{:S(2)}) collective-permute-start(bf16[256,1024]{1,0:T(8,128)(2,1)S(1)} %get-tuple-element.365.refs_0_.refs_3_), channel_id=1, source_target_pairs={{0,1},{1,0},{2,3},{3,2},{4,5},{5,4},{6,7},{7,6},{8,9},{9,8},{10,11... | collective-permute-start | bytes 1572872 | tf_op jit(solution)/shard_map/ppermute | solution.py:115
  144.7 21.1 %collective-permute-start.31 = (bf16[256,1024]{1,0:T(8,128)(2,1)S(1)}, bf16[256,1024]{1,0:T(8,128)(2,1)S(1)}, u32[]{:S(2)}, u32[]{:S(2)}) collective-permute-start(bf16[256,1024]{1,0:T(8,128)(2,1)S(1)} %get-tuple-element.365.refs_0_.refs_3_), channel_id=1, source_target_pairs={{0,2},{1,3},{2,0},{3,1},{4,6},{5,7},{6,4},{7,5},{8,10},{9,11},{10,... | collective-permute-start | bytes 1572872 | tf_op jit(solution)/shard_map/ppermute | solution.py:115
  155.5 18.3 %collective-permute-start.35 = (bf16[256,1024]{1,0:T(8,128)(2,1)S(1)}, bf16[256,1024]{1,0:T(8,128)(2,1)S(1)}, u32[]{:S(2)}, u32[]{:S(2)}) collective-permute-start(bf16[256,1024]{1,0:T(8,128)(2,1)S(1)} %get-tuple-element.407), channel_id=1, source_target_pairs={{0,8},{4,12},{8,0},{12,4},{16,24},{20,28},{24,16},{28,20},{1,9},{5... | collective-permute-start | bytes 1572872 | tf_op jit(solution)/shard_map/ppermute | solution.py:115
  157.0 24.4 %collective-permute-start.37 = (bf16[512,1024]{1,0:T(8,128)(2,1)S(1)}, bf16[512,1024]{1,0:T(8,128)(2,1)S(1)}, u32[]{:S(2)}, u32[]{:S(2)}) collective-permute-start(bf16[512,1024]{1,0:T(8,128)(2,1)S(1)} %get-tuple-element.416), channel_id=1, source_target_pairs={{0,4},{4,0},{8,12},{12,8},{16,20},{20,16},{24,28},{28,24},{1,5},{5... | collective-permute-start | bytes 3145736 | tf_op jit(solution)/shard_map/ppermute | solution.py:115
  165.8 4.2 %collective-permute-start.33 = (bf16[256,1024]{1,0:T(8,128)(2,1)S(1)}, bf16[256,1024]{1,0:T(8,128)(2,1)S(1)}, u32[]{:S(2)}, u32[]{:S(2)}) collective-permute-start(bf16[256,1024]{1,0:T(8,128)(2,1)S(1)} %get-tuple-element.385.refs_0_.refs_5_), channel_id=1, source_target_pairs={{0,1},{1,0},{2,3},{3,2},{4,5},{5,4},{6,7},{7,6},{8,9},{9,8},{10,11... | collective-permute-start | bytes 1572872 | tf_op jit(solution)/shard_map/ppermute | solution.py:115
  166.4 43.2 %collective-permute-start.42 = (bf16[896,512]{1,0:T(8,128)(2,1)S(1)}, bf16[896,512]{1,0:T(8,128)(2,1)S(1)}, u32[]{:S(2)}, u32[]{:S(2)}) collective-permute-start(bf16[896,512]{1,0:T(8,128)(2,1)S(1)} %get-tuple-element.428), channel_id=1, source_target_pairs={{0,2},{1,3},{2,0},{3,1},{4,6},{5,7},{6,4},{7,5},{8,10},{9,11},{10,... | collective-permute-start | bytes 2752520 | tf_op jit(solution)/shard_map/ppermute | solution.py:115
  173.8 7.1 %collective-permute-start.34 = (bf16[256,1024]{1,0:T(8,128)(2,1)S(1)}, bf16[256,1024]{1,0:T(8,128)(2,1)S(1)}, u32[]{:S(2)}, u32[]{:S(2)}) collective-permute-start(bf16[256,1024]{1,0:T(8,128)(2,1)S(1)} %get-tuple-element.401), channel_id=1, source_target_pairs={{0,1},{1,0},{2,3},{3,2},{4,5},{5,4},{6,7},{7,6},{8,9},{9,8},{10,11... | collective-permute-start | bytes 1572872 | tf_op jit(solution)/shard_map/ppermute | solution.py:115
  173.9 15.4 %collective-permute-start.39 = (bf16[128,1024]{1,0:T(8,128)(2,1)S(1)}, bf16[128,1024]{1,0:T(8,128)(2,1)S(1)}, u32[]{:S(2)}, u32[]{:S(2)}) collective-permute-start(bf16[128,1024]{1,0:T(8,128)(2,1)S(1)} %get-tuple-element.421), channel_id=1, source_target_pairs={{0,16},{4,20},{8,24},{12,28},{16,0},{20,4},{24,8},{28,12},{1,17},{... | collective-permute-start | bytes 786440 | tf_op jit(solution)/shard_map/ppermute | solution.py:115
  180.5 33.2 %collective-permute-start.40 = (bf16[512,1024]{1,0:T(8,128)(2,1)S(1)}, bf16[512,1024]{1,0:T(8,128)(2,1)S(1)}, u32[]{:S(2)}, u32[]{:S(2)}) collective-permute-start(bf16[512,1024]{1,0:T(8,128)(2,1)S(1)} %get-tuple-element.426), channel_id=1, source_target_pairs={{0,4},{4,0},{8,12},{12,8},{16,20},{20,16},{24,28},{28,24},{1,5},{5... | collective-permute-start | bytes 3145736 | tf_op jit(solution)/shard_map/ppermute | solution.py:115
  185.5 20.6 %collective-permute-start.38 = (bf16[256,1024]{1,0:T(8,128)(2,1)S(1)}, bf16[256,1024]{1,0:T(8,128)(2,1)S(1)}, u32[]{:S(2)}, u32[]{:S(2)}) collective-permute-start(bf16[256,1024]{1,0:T(8,128)(2,1)S(1)} %get-tuple-element.419), channel_id=1, source_target_pairs={{0,8},{4,12},{8,0},{12,4},{16,24},{20,28},{24,16},{28,20},{1,9},{5... | collective-permute-start | bytes 1572872 | tf_op jit(solution)/shard_map/ppermute | solution.py:115
  185.9 21.1 %collective-permute-start.36 = (bf16[256,1024]{1,0:T(8,128)(2,1)S(1)}, bf16[256,1024]{1,0:T(8,128)(2,1)S(1)}, u32[]{:S(2)}, u32[]{:S(2)}) collective-permute-start(bf16[256,1024]{1,0:T(8,128)(2,1)S(1)} %get-tuple-element.411), channel_id=1, source_target_pairs={{0,2},{1,3},{2,0},{3,1},{4,6},{5,7},{6,4},{7,5},{8,10},{9,11},{10,... | collective-permute-start | bytes 1572872 | tf_op jit(solution)/shard_map/ppermute | solution.py:115
  189.4 20.8 %collective-permute-start.41 = (bf16[128,1024]{1,0:T(8,128)(2,1)S(1)}, bf16[128,1024]{1,0:T(8,128)(2,1)S(1)}, u32[]{:S(2)}, u32[]{:S(2)}) collective-permute-start(bf16[128,1024]{1,0:T(8,128)(2,1)S(1)} %get-tuple-element.427.refs_0_), channel_id=1, source_target_pairs={{0,16},{4,20},{8,24},{12,28},{16,0},{20,4},{24,8},{28,12},{1,17},{... | collective-permute-start | bytes 786440 | tf_op jit(solution)/shard_map/ppermute | solution.py:115
  206.3 14.0 %collective-permute-start.47 = (bf16[128,1024]{1,0:T(8,128)(2,1)S(1)}, bf16[128,1024]{1,0:T(8,128)(2,1)S(1)}, u32[]{:S(2)}, u32[]{:S(2)}) collective-permute-start(bf16[128,1024]{1,0:T(8,128)(2,1)S(1)} %get-tuple-element.439), channel_id=1, source_target_pairs={{0,16},{4,20},{8,24},{12,28},{16,0},{20,4},{24,8},{28,12},{1,17},{... | collective-permute-start | bytes 786440 | tf_op jit(solution)/shard_map/ppermute | solution.py:115
  210.2 20.4 %collective-permute-start.46 = (bf16[256,1024]{1,0:T(8,128)(2,1)S(1)}, bf16[256,1024]{1,0:T(8,128)(2,1)S(1)}, u32[]{:S(2)}, u32[]{:S(2)}) collective-permute-start(bf16[256,1024]{1,0:T(8,128)(2,1)S(1)} %get-tuple-element.437.refs_0_), channel_id=1, source_target_pairs={{0,8},{4,12},{8,0},{12,4},{16,24},{20,28},{24,16},{28,20},{1,9},{5... | collective-permute-start | bytes 1572872 | tf_op jit(solution)/shard_map/ppermute | solution.py:115
  212.3 20.8 %collective-permute-start.44 = (bf16[896,512]{1,0:T(8,128)(2,1)S(1)}, bf16[896,512]{1,0:T(8,128)(2,1)S(1)}, u32[]{:S(2)}, u32[]{:S(2)}) collective-permute-start(bf16[896,512]{1,0:T(8,128)(2,1)S(1)} %get-tuple-element.435), channel_id=1, source_target_pairs={{0,2},{1,3},{2,0},{3,1},{4,6},{5,7},{6,4},{7,5},{8,10},{9,11},{10,... | collective-permute-start | bytes 2752520 | tf_op jit(solution)/shard_map/ppermute | solution.py:115
  213.3 21.3 %collective-permute-start.45 = (bf16[896,512]{1,0:T(8,128)(2,1)S(1)}, bf16[896,512]{1,0:T(8,128)(2,1)S(1)}, u32[]{:S(2)}, u32[]{:S(2)}) collective-permute-start(bf16[896,512]{1,0:T(8,128)(2,1)S(1)} %get-tuple-element.436), channel_id=1, source_target_pairs={{0,4},{4,0},{8,12},{12,8},{16,20},{20,16},{24,28},{28,24},{1,5},{5... | collective-permute-start | bytes 2752520 | tf_op jit(solution)/shard_map/ppermute | solution.py:115
  217.6 29.9 %collective-permute-start.43 = (bf16[256,1024]{1,0:T(8,128)(2,1)S(1)}, bf16[256,1024]{1,0:T(8,128)(2,1)S(1)}, u32[]{:S(2)}, u32[]{:S(2)}) collective-permute-start(bf16[256,1024]{1,0:T(8,128)(2,1)S(1)} %get-tuple-element.434), channel_id=1, source_target_pairs={{0,8},{4,12},{8,0},{12,4},{16,24},{20,28},{24,16},{28,20},{1,9},{5... | collective-permute-start | bytes 1572872 | tf_op jit(solution)/shard_map/ppermute | solution.py:115
  220.3 30.3 %collective-permute-start.50 = (f32[24,1024]{1,0:T(8,128)S(1)}, f32[24,1024]{1,0:T(8,128)S(1)}, u32[]{:S(2)}, u32[]{:S(2)}) collective-permute-start(f32[24,1024]{1,0:T(8,128)S(1)} %get-tuple-element.448.refs_0_), channel_id=1, source_target_pairs={{0,1},{1,0},{2,3},{3,2},{4,5},{5,4},{6,7},{7,6},{8,9},{9,8},{10,11... | collective-permute-start | bytes 294920 | tf_op jit(solution)/shard_map/ppermute | solution.py:115
  230.6 17.4 %collective-permute-start.51 = (bf16[128,1024]{1,0:T(8,128)(2,1)S(1)}, bf16[128,1024]{1,0:T(8,128)(2,1)S(1)}, u32[]{:S(2)}, u32[]{:S(2)}) collective-permute-start(bf16[128,1024]{1,0:T(8,128)(2,1)S(1)} %get-tuple-element.449.refs_0_), channel_id=1, source_target_pairs={{0,16},{4,20},{8,24},{12,28},{16,0},{20,4},{24,8},{28,12},{1,17},{... | collective-permute-start | bytes 786440 | tf_op jit(solution)/shard_map/ppermute | solution.py:115
  233.1 44.9 %collective-permute-start.54 = (bf16[512,1024]{1,0:T(8,128)(2,1)S(1)}, bf16[512,1024]{1,0:T(8,128)(2,1)S(1)}, u32[]{:S(2)}, u32[]{:S(2)}) collective-permute-start(bf16[512,1024]{1,0:T(8,128)(2,1)S(1)} %get-tuple-element.456.refs_1_), channel_id=1, source_target_pairs={{0,4},{4,0},{8,12},{12,8},{16,20},{20,16},{24,28},{28,24},{1,5},{5... | collective-permute-start | bytes 3145736 | tf_op jit(solution)/shard_map/ppermute | solution.py:115
  235.6 27.3 %collective-permute-start.49 = (bf16[448,512]{1,0:T(8,128)(2,1)S(1)}, bf16[448,512]{1,0:T(8,128)(2,1)S(1)}, u32[]{:S(2)}, u32[]{:S(2)}) collective-permute-start(bf16[448,512]{1,0:T(8,128)(2,1)S(1)} %get-tuple-element.447), channel_id=1, source_target_pairs={{0,8},{4,12},{8,0},{12,4},{16,24},{20,28},{24,16},{28,20},{1,9},{5... | collective-permute-start | bytes 1376264 | tf_op jit(solution)/shard_map/ppermute | solution.py:115
  247.6 15.4 %collective-permute-start.48 = (bf16[128,1024]{1,0:T(8,128)(2,1)S(1)}, bf16[128,1024]{1,0:T(8,128)(2,1)S(1)}, u32[]{:S(2)}, u32[]{:S(2)}) collective-permute-start(bf16[128,1024]{1,0:T(8,128)(2,1)S(1)} %get-tuple-element.445), channel_id=1, source_target_pairs={{0,16},{4,20},{8,24},{12,28},{16,0},{20,4},{24,8},{28,12},{1,17},{... | collective-permute-start | bytes 786440 | tf_op jit(solution)/shard_map/ppermute | solution.py:115
  248.1 29.8 %collective-permute-start.55 = (bf16[256,1024]{1,0:T(8,128)(2,1)S(1)}, bf16[256,1024]{1,0:T(8,128)(2,1)S(1)}, u32[]{:S(2)}, u32[]{:S(2)}) collective-permute-start(bf16[256,1024]{1,0:T(8,128)(2,1)S(1)} %get-tuple-element.457.refs_0_), channel_id=1, source_target_pairs={{0,8},{4,12},{8,0},{12,4},{16,24},{20,28},{24,16},{28,20},{1,9},{5... | collective-permute-start | bytes 1572872 | tf_op jit(solution)/shard_map/ppermute | solution.py:115
  250.7 29.7 %collective-permute-start.53 = (f32[24,1024]{1,0:T(8,128)S(1)}, f32[24,1024]{1,0:T(8,128)S(1)}, u32[]{:S(2)}, u32[]{:S(2)}) collective-permute-start(f32[24,1024]{1,0:T(8,128)S(1)} %get-tuple-element.455.refs_0_), channel_id=1, source_target_pairs={{0,2},{1,3},{2,0},{3,1},{4,6},{5,7},{6,4},{7,5},{8,10},{9,11},{10,... | collective-permute-start | bytes 294920 | tf_op jit(solution)/shard_map/ppermute | solution.py:115
  263.1 20.4 %collective-permute-start.52 = (bf16[128,1024]{1,0:T(8,128)(2,1)S(1)}, bf16[128,1024]{1,0:T(8,128)(2,1)S(1)}, u32[]{:S(2)}, u32[]{:S(2)}) collective-permute-start(bf16[128,1024]{1,0:T(8,128)(2,1)S(1)} %get-tuple-element.454.refs_0_), channel_id=1, source_target_pairs={{0,16},{4,20},{8,24},{12,28},{16,0},{20,4},{24,8},{28,12},{1,17},{... | collective-permute-start | bytes 786440 | tf_op jit(solution)/shard_map/ppermute | solution.py:115
  263.6 22.6 %collective-permute-start.58 = (bf16[224,512]{1,0:T(8,128)(2,1)S(1)}, bf16[224,512]{1,0:T(8,128)(2,1)S(1)}, u32[]{:S(2)}, u32[]{:S(2)}) collective-permute-start(bf16[224,512]{1,0:T(8,128)(2,1)S(1)} %get-tuple-element.465), channel_id=1, source_target_pairs={{0,16},{4,20},{8,24},{12,28},{16,0},{20,4},{24,8},{28,12},{1,17},{... | collective-permute-start | bytes 688136 | tf_op jit(solution)/shard_map/ppermute | solution.py:115
  277.9 26.6 %collective-permute-start.61 = (bf16[512,1024]{1,0:T(8,128)(2,1)S(1)}, bf16[512,1024]{1,0:T(8,128)(2,1)S(1)}, u32[]{:S(2)}, u32[]{:S(2)}) collective-permute-start(bf16[512,1024]{1,0:T(8,128)(2,1)S(1)} %get-tuple-element.471.refs_1_), channel_id=1, source_target_pairs={{0,4},{4,0},{8,12},{12,8},{16,20},{20,16},{24,28},{28,24},{1,5},{5... | collective-permute-start | bytes 3145736 | tf_op jit(solution)/shard_map/ppermute | solution.py:115
  280.3 24.0 %collective-permute-start.57 = (f32[24,1024]{1,0:T(8,128)S(1)}, f32[24,1024]{1,0:T(8,128)S(1)}, u32[]{:S(2)}, u32[]{:S(2)}) collective-permute-start(f32[24,1024]{1,0:T(8,128)S(1)} %get-tuple-element.463.refs_0_), channel_id=1, source_target_pairs={{0,4},{4,0},{8,12},{12,8},{16,20},{20,16},{24,28},{28,24},{1,5},{5... | collective-permute-start | bytes 294920 | tf_op jit(solution)/shard_map/ppermute | solution.py:115
  283.6 20.8 %collective-permute-start.56 = (bf16[256,1024]{1,0:T(8,128)(2,1)S(1)}, bf16[256,1024]{1,0:T(8,128)(2,1)S(1)}, u32[]{:S(2)}, u32[]{:S(2)}) collective-permute-start(bf16[256,1024]{1,0:T(8,128)(2,1)S(1)} %get-tuple-element.462.refs_0_), channel_id=1, source_target_pairs={{0,8},{4,12},{8,0},{12,4},{16,24},{20,28},{24,16},{28,20},{1,9},{5... | collective-permute-start | bytes 1572872 | tf_op jit(solution)/shard_map/ppermute | solution.py:115
  286.2 20.6 %collective-permute-start.60 = (bf16[224,512]{1,0:T(8,128)(2,1)S(1)}, bf16[224,512]{1,0:T(8,128)(2,1)S(1)}, u32[]{:S(2)}, u32[]{:S(2)}) collective-permute-start(bf16[224,512]{1,0:T(8,128)(2,1)S(1)} %get-tuple-element.470.refs_0_), channel_id=1, source_target_pairs={{0,16},{4,20},{8,24},{12,28},{16,0},{20,4},{24,8},{28,12},{1,17},{... | collective-permute-start | bytes 688136 | tf_op jit(solution)/shard_map/ppermute | solution.py:115
  304.3 4.7 %collective-permute-start.63 = (f32[24,1024]{1,0:T(8,128)S(1)}, f32[24,1024]{1,0:T(8,128)S(1)}, u32[]{:S(2)}, u32[]{:S(2)}) collective-permute-start(f32[24,1024]{1,0:T(8,128)S(1)} %get-tuple-element.475.refs_0_), channel_id=1, source_target_pairs={{0,8},{4,12},{8,0},{12,4},{16,24},{20,28},{24,16},{28,20},{1,9},{5... | collective-permute-start | bytes 294920 | tf_op jit(solution)/shard_map/ppermute | solution.py:115
  309.0 6.5 %collective-permute-start.64 = (f32[24,1024]{1,0:T(8,128)S(1)}, f32[24,1024]{1,0:T(8,128)S(1)}, u32[]{:S(2)}, u32[]{:S(2)}) collective-permute-start(f32[24,1024]{1,0:T(8,128)S(1)} %get-tuple-element.477.refs_0_.refs_1_), channel_id=1, source_target_pairs={{0,16},{4,20},{8,24},{12,28},{16,0},{20,4},{24,8},{28,12},{1,17},{... | collective-permute-start | bytes 294920 | tf_op jit(solution)/shard_map/ppermute | solution.py:115
  309.6 26.1 %collective-permute-start.59 = (bf16[512,1024]{1,0:T(8,128)(2,1)S(1)}, bf16[512,1024]{1,0:T(8,128)(2,1)S(1)}, u32[]{:S(2)}, u32[]{:S(2)}) collective-permute-start(bf16[512,1024]{1,0:T(8,128)(2,1)S(1)} %get-tuple-element.469.refs_1_), channel_id=1, source_target_pairs={{0,4},{4,0},{8,12},{12,8},{16,20},{20,16},{24,28},{28,24},{1,5},{5... | collective-permute-start | bytes 3145736 | tf_op jit(solution)/shard_map/ppermute | solution.py:115
  309.9 11.5 %collective-permute-start.62 = (bf16[448,512]{1,0:T(8,128)(2,1)S(1)}, bf16[448,512]{1,0:T(8,128)(2,1)S(1)}, u32[]{:S(2)}, u32[]{:S(2)}) collective-permute-start(bf16[448,512]{1,0:T(8,128)(2,1)S(1)} %get-tuple-element.474.refs_0_), channel_id=1, source_target_pairs={{0,8},{4,12},{8,0},{12,4},{16,24},{20,28},{24,16},{28,20},{1,9},{5... | collective-permute-start | bytes 1376264 | tf_op jit(solution)/shard_map/ppermute | solution.py:115
  321.5 29.8 %collective-permute-start.65 = (bf16[896,512]{1,0:T(8,128)(2,1)S(1)}, bf16[896,512]{1,0:T(8,128)(2,1)S(1)}, u32[]{:S(2)}, u32[]{:S(2)}) collective-permute-start(bf16[896,512]{1,0:T(8,128)(2,1)S(1)} %get-tuple-element.491.refs_1_), channel_id=1, source_target_pairs={{0,4},{4,0},{8,12},{12,8},{16,20},{20,16},{24,28},{28,24},{1,5},{5... | collective-permute-start | bytes 2752520 | tf_op jit(solution)/shard_map/ppermute | solution.py:115
  (73 other events, 255.4 us)
